TPU v7x, 128 devices: a whole 4x4x4 slice. The times are simulated.
128 devices in a mesh: rows: 32 (over y_hi, x, z), rep: 4 (over y_lo, core).
Axes of the slice: x: 4, y: 4 (y_hi: 2, y_lo: 2; y = y_hi * 2 + y_lo), z: 4, core: 2. Of those that a mesh axis runs over, the one named last changes fastest.
Arguments:
- features: bfloat16 [65536, 256], P('rows'), may hold values from -6 to 6
- weight: bfloat16 [256, 256], replicated, may hold values from -0.375 to 0.375
- bias: float32 [256], replicated, may hold values from -3 to 3
- cotangent: bfloat16 [65536, 256], P(('rows', 'rep')), may hold values from -6 to 6
- tile_vals: bfloat16 [32, 4, 32, 4, 128, 128], P('rows', 'rep'), may hold values from -0.09375 to 0.09375
- tile_rows: int32 [32, 4, 32, 4], P('rows', 'rep'), may hold values from 0 to 15
- tile_pick: int32 [32, 4, 32, 4], P('rows', 'rep'), may hold values from 0 to 1
- tile_count: int32 [32, 4, 32], P('rows', 'rep'), may hold values from 0 to 4, as said below
- pull_cols: int32 [32, 4, 32, 2], P('rows', 'rep'), may hold values from 0 to 3
Outputs:
- activations: bfloat16 [65536, 256], P(('rows', 'rep'))
- feature_grads: float32 [65536, 256], P(('rows', 'rep'))
- weight_grad: float32 [256, 256], replicated
- bias_grad: float32 [256], replicated
Inputs may be any that keep to these rules, and one draw needn't show every extreme that they name: Only the first tile_count slots of a row block, column quarter and section are live; the others are padding. Some entry equals 4 in every draw.
All inputs are finite; a program needn't handle non-finite values.
Results may differ from a plain program's by a relative error of at most 0.0052.
Values may be sent and summed in bfloat16 or wider, within the bound.
A program may use at most 128 MiB of HBM per device.

v0:
```python
import jax
import jax.numpy as jnp
from jax import lax
from jax.sharding import PartitionSpec as P


def silu_slope(pre):
    sig = jax.nn.sigmoid(pre)
    return sig * (1.0 + pre * (1.0 - sig))


def tile_products(values, blocks):
    return jnp.einsum("kab,kbf->kaf", values, blocks, preferred_element_type=jnp.float32)


def tile_transposed(values, blocks):
    return jnp.einsum("kba,kbf->kaf", values, blocks, preferred_element_type=jnp.float32)


def spread_rows(products, placing):
    return jnp.einsum("kr,kaf->raf", placing, products, precision=lax.Precision.HIGHEST)


def local(
    features, weight, bias, cotangent, tile_vals, tile_rows, tile_pick, tile_count, pull_cols
):
    node_dev, width_in = features.shape
    sections = tile_vals.shape[2]
    slots = tile_vals.shape[3]
    tile = tile_vals.shape[4]
    replicas = lax.axis_size("rep")
    replica = lax.axis_index("rep")
    quarter = node_dev // replicas
    col_tiles = quarter // tile
    row_tiles = node_dev // tile
    values = tile_vals[0, 0].reshape(sections * slots, tile, tile)
    row_ids = tile_rows[0, 0]
    picks = tile_pick[0, 0]
    wanted = pull_cols[0, 0]
    live = (jnp.arange(slots)[None, :] < tile_count[0, 0][:, None]).astype(jnp.float32)
    row_hot = (row_ids[:, :, None] == jnp.arange(row_tiles)[None, None, :]).astype(
        jnp.float32
    ) * live[:, :, None]
    col_ids = jnp.take_along_axis(wanted, picks, axis=1)
    own_quarter = lax.dynamic_slice_in_dim(features, replica * quarter, quarter, 0)
    piece = lax.all_gather(own_quarter, "rows", axis=0, tiled=True)
    number = piece.shape[0] // quarter
    part_values = values
    part_cols = col_ids
    part_hot = row_hot.reshape(number * slots, row_tiles)
    index = (jnp.arange(number)[:, None] * col_tiles + part_cols).reshape(-1)
    blocks = jnp.take(piece.reshape(number * col_tiles, tile, width_in), index, axis=0)
    partial_value = spread_rows(tile_products(part_values, blocks), part_hot)
    partial_value = partial_value.reshape(node_dev, width_in)
    total = lax.psum(partial_value, "rep")
    aggregated = total.astype(jnp.bfloat16)
    pre = jnp.dot(aggregated, weight, preferred_element_type=jnp.float32) + bias
    grad_rows = lax.all_gather(cotangent, "rep", axis=0, tiled=True)
    slope = (grad_rows.astype(jnp.float32) * silu_slope(pre)).astype(jnp.bfloat16)
    back = lax.dot_general(
        slope, weight, (((1,), (1,)), ((), ())), preferred_element_type=jnp.float32
    ).astype(jnp.bfloat16)
    own_pre = lax.dynamic_slice_in_dim(pre, replica * quarter, quarter, 0)
    activations = jax.nn.silu(own_pre).astype(jnp.bfloat16)
    mine_agg = lax.dynamic_slice_in_dim(aggregated, replica * quarter, quarter, 0)
    mine_slope = lax.dynamic_slice_in_dim(slope, replica * quarter, quarter, 0)
    weight_part = lax.dot_general(
        mine_agg, mine_slope, (((0,), (0,)), ((), ())), preferred_element_type=jnp.float32
    )
    bias_part = jnp.sum(mine_slope.astype(jnp.float32), axis=0)
    weight_grad, bias_grad = lax.psum((weight_part, bias_part), ("rows", "rep"))
    sources = jnp.take(back.reshape(row_tiles, tile, width_in), row_ids.reshape(-1), axis=0)
    number = quarter * lax.axis_size("rows") // quarter
    part_values = values
    part_cols = col_ids
    terms = tile_transposed(part_values, sources).reshape(number, slots, tile, width_in)
    placing = (part_cols[:, :, None] == jnp.arange(col_tiles)[None, None, :]).astype(
        jnp.float32
    ) * live[:, :, None]
    placed = jnp.einsum("stq,staf->sqaf", placing, terms, precision=lax.Precision.HIGHEST)
    feature_grads = lax.psum_scatter(
        placed.reshape(quarter * lax.axis_size("rows"), width_in),
        "rows",
        scatter_dimension=0,
        tiled=True,
    )
    return (activations, feature_grads, weight_grad, bias_grad)


def solution(mesh):
    in_specs = (
        P("rows", None),
        P(),
        P(),
        P(("rows", "rep"), None),
        P("rows", "rep", None, None, None, None),
        P("rows", "rep", None, None),
        P("rows", "rep", None, None),
        P("rows", "rep", None),
        P("rows", "rep", None, None),
    )
    out_specs = (P(("rows", "rep"), None), P(("rows", "rep"), None), P(), P())
    return jax.shard_map(local, mesh=mesh, in_specs=in_specs, out_specs=out_specs, check_vma=False)
```

profile of v0, /device:TPU:0, one launch (start us, length us, event | category | flops | bytes accessed | tf_op | source)
XLA Modules:
  0.0 590.3 jit_solution(4130583681142961473)
XLA Ops:
  7.2 1.2 copy-done
  8.4 0.7 constant_dynamic-slice_fusion
  9.2 0.7 all-gather.5.cloned.1.call-update
  10.0 0.1 add.152
  10.1 0.1 add.143
  10.2 0.8 copy.21
  11.1 0.1 reshape_squeeze.7
  11.2 0.7 fusion.27
  11.9 0.8 copy.22
  12.8 0.1 squeeze.12
  13.0 0.1 reshape.250
  13.1 0.7 fusion.19
  14.0 1.5 gather_fusion.2
  15.8 102.7 %all-gather.3.cloned.1.call-done = bf16[16384,256]{1,0:T(8,128)(2,1)} async-done(((bf16[512,256]{1,0:T(8,128)(2,1)}), bf16[16384,256]{1,0:T(8,128)(2,1)}) %all-gather.3.cloned.1.call-update) | async-done | bytes 8388624 | tf_op jit(solution)/shard_map/all_gather | solution.py:46
  118.5 10.1 %gather_fusion = bf16[128,128,256]{2,1,0:T(8,128)(2,1)} fusion(bf16[128,128,256]{2,1,0:T(8,128)(2,1)} %bitcast.58, s32[1024]{0:T(1024)S(1)} %pad_clamp_fusion.1), kind=kCustom, calls=%fused_computation | custom fusion | bytes 16777728 | tf_op jit(solution)/shard_map/jit(_take)/gather | solution.py:52
  128.6 13.2 %fusion.4 = f32[128,256,128]{2,1,0:T(8,128)} fusion(bf16[128,128,128]{2,1,0:T(8,128)(2,1)} %bitcast.56, bf16[128,128,256]{2,1,0:T(8,128)(2,1)} %gather_fusion, pred[128]{0:T(512)(128)(4,1)S(1)} %compare_and_fusion.1), kind=kOutput, calls=%fused_computation.7 | convolution fusion | flops 1077936128 | bytes 29360256 | tf_op jit(solution)/shard_map/kab,kbf->kaf/dot_general | solution.py:13
  141.7 17.7 %copy.32 = f32[128,256,128]{1,0,2:T(8,128)} copy(f32[128,256,128]{2,1,0:T(8,128)} %fusion.4) | data formatting | bytes 33554432 | tf_op jit(solution)/shard_map/kab,kbf->kaf/dot_general | solution.py:13
  159.4 10.9 %fusion = f32[16,128,256]{2,0,1:T(8,128)S(1)} fusion(f32[128,256,128]{1,0,2:T(8,128)} %copy.32, f32[128]{0:T(128)S(1)} %reshape.233, s32[128]{0:T(128)S(1)} %eq.29), kind=kOutput, calls=%fused_computation.3 | convolution fusion | flops 805310464 | bytes 18875392 | tf_op jit(solution)/shard_map/kr,kaf->raf/dot_general | solution.py:21
  170.4 1.2 copy.25
  171.6 40.8 %all-reduce.4 = bf16[2048,256]{1,0:T(8,128)(2,1)S(1)} all-reduce(f32[2048,256]{1,0:T(8,128)S(1)} %bitcast.59), channel_id=1, replica_groups=mesh['rows'=32,'rep'=4] {'rep'}, use_global_device_ids=true, to_apply=%region_0.0 | all-reduce | flops 524288 | bytes 3145728 | tf_op jit(solution)/shard_map/psum | solution.py:55
  212.4 3.5 multiply_convert_fusion
  216.0 1.0 fusion.10
  216.9 0.5 convolution_convert_fusion
  217.5 6.6 %gather_fusion.1 = bf16[128,128,256]{2,1,0:T(8,128)(2,1)} fusion(bf16[16,128,256]{2,1,0:T(8,128)(2,1)S(1)} %bitcast.53, s32[1024]{0:T(1024)S(1)} %pad_clamp_fusion), kind=kCustom, calls=%fused_computation.1 | custom fusion | bytes 16777728 | tf_op jit(solution)/shard_map/jit(_take)/gather | solution.py:72
  224.0 12.9 %fusion.2 = f32[128,256,128]{2,1,0:T(8,128)} fusion(bf16[128,128,128]{2,1,0:T(8,128)(2,1)} %bitcast.57, bf16[128,128,256]{2,1,0:T(8,128)(2,1)} %gather_fusion.1, pred[128]{0:T(512)(128)(4,1)S(1)} %compare_and_fusion), kind=kOutput, calls=%fused_computation.5 | convolution fusion | flops 1077936128 | bytes 29360256 | tf_op jit(solution)/shard_map/kba,kbf->kaf/dot_general | solution.py:17
  236.9 19.2 %copy.30 = f32[32,4,128,256]{3,1,2,0:T(4,128)} copy(f32[32,4,128,256]{2,3,1,0:T(8,128)} %bitcast.55) | data formatting | bytes 33554432 | tf_op jit(solution)/shard_map/reshape | solution.py:76
  256.1 32.5 %fusion.13 = f32[32,4,128,256]{3,1,2,0:T(4,128)S(1)} fusion(f32[32,4,128,256]{3,1,2,0:T(4,128)} %copy.30, f32[32,4]{1,0:T(8,128)S(1)} %fusion.19, s32[32,4]{1,0:T(8,128)S(1)} %copy.27), kind=kOutput, calls=%fused_computation.21 | convolution fusion | flops 201327616 | bytes 33555456 | tf_op jit(solution)/shard_map/stq,staf->sqaf/dot_general | solution.py:80
  288.7 6.7 %copy.31 = f32[32,4,128,256]{3,2,1,0:T(8,128)} copy(f32[32,4,128,256]{3,1,2,0:T(4,128)S(1)} %fusion.13) | data formatting | bytes 33554432 | tf_op jit(solution)/shard_map/stq,staf->sqaf/dot_general | solution.py:80
  295.4 65.2 %psum.23 = f32[256]{0:T(256)} all-reduce(f32[256]{0:T(256)S(1)} %convert_reduce_fusion), channel_id=1, replica_groups=mesh['rows'=32,'rep'=4] {'rows','rep'}, use_global_device_ids=true, to_apply=%region_4.5 | all-reduce | flops 256 | bytes 2048 | tf_op jit(solution)/shard_map/psum | solution.py:71
  360.7 1.9 multiply_convert_fusion.1
  362.6 219.5 %reduce-scatter.2.cloned.1.call-done = f32[512,256]{1,0:T(8,128)} async-done(((f32[16384,256]{1,0:T(8,128)}), f32[512,256]{1,0:T(8,128)}) %reduce-scatter.2.cloned.1.call-update) | async-done | bytes 524304 | tf_op jit(solution)/shard_map/reduce_scatter | solution.py:81
  582.1 1.7 copy.38
  (37 shorter events, 1.1 us)
Async XLA Ops:
  7.2 1.2 copy-start
  7.2 6.8 %copy-start.2 = (s32[1,1,32,2]{2,3,1,0:T(2,128)S(1)}, s32[1,1,32,2]{2,3,1,0:T(2,128)}, u32[]{:S(2)}) copy-start(s32[1,1,32,2]{2,3,1,0:T(2,128)} %param.17) | copy-start | bytes 772
  7.2 111.3 %all-gather.3.cloned.1.call-start = ((), (), s32[]{:S(2)}) async-start(), calls=%async_computation.1 | async-start | bytes 8650752 | tf_op jit(solution)/shard_map/all_gather | solution.py:46
  9.1 203.3 %all-gather.5.cloned.1.call-start = ((), (), s32[]{:S(2)}) async-start(), calls=%async_computation.2 | async-start | bytes 1310720 | tf_op jit(solution)/shard_map/all_gather | solution.py:58
  9.9 352.7 %all-reduce.3.cloned.1.call-start = ((), (), s32[]{:S(2)}) async-start(), calls=%async_computation.4 | async-start | bytes 524288 | tf_op jit(solution)/shard_map/psum | solution.py:71
  14.0 1.7 copy-start.4
  159.4 53.0 %copy-start.3 = (bf16[256,256]{1,0:T(8,128)(2,1)S(1)}, bf16[256,256]{1,0:T(8,128)(2,1)}, u32[]{:S(2)}) copy-start(bf16[256,256]{1,0:T(8,128)(2,1)} %param.10) | copy-start | bytes 393220
  159.4 53.0 %copy-start.5 = (f32[256]{0:T(256)S(1)}, f32[256]{0:T(256)}, u32[]{:S(2)}) copy-start(f32[256]{0:T(256)} %param.11) | copy-start | bytes 3076
  217.4 364.7 %reduce-scatter.2.cloned.1.call-start = ((), (), s32[]{:S(2)}) async-start(), calls=%async_computation.3 | async-start | bytes 17301504 | tf_op jit(solution)/shard_map/reduce_scatter | solution.py:81
  295.3 288.4 %copy-start.1 = (bf16[2048,256]{1,0:T(8,128)(2,1)S(1)}, bf16[2048,256]{1,0:T(8,128)(2,1)}, u32[]{:S(2)}) copy-start(bf16[2048,256]{1,0:T(8,128)(2,1)} %param.9) | copy-start | bytes 3145732
Sparse Core Ops, SparseCore 0:
  11.7 106.7 all-gather.2
  120.2 18.3 all-gather.4
  217.5 139.8 all-reduce.2
  360.3 221.7 reduce-scatter.1
where the time goes:
time: 591 us; the launch traced here: 590 us
  waiting for transfers between devices  323 us (55%)
  blocking collectives  106 us (18%)
  matrix products  74.4 us (13%)
  local copies, waits for them, and re-layouts  69.3 us (12%)
  between operations  14 us (2%)
    reduce_scatter x1, waiting for transfers between devices, local(): lax.psum_scatter(placed.reshape(quarter * lax.axis_size('rows'), width_in...  220 us
    all_gather x1, waiting for transfers between devices, local(): piece = lax.all_gather(own_quarter, 'rows', axis=0, tiled=True)  103 us
    psum x1, blocking collectives, local(): weight_grad, bias_grad = lax.psum((weight_part, bias_part), ('rows', 'rep'))  65.2 us
    psum x1, blocking collectives, local(): total = lax.psum(partial_value, 'rep')  40.8 us
    dot_general x1, matrix products, local(): jnp.einsum('stq,staf->sqaf', placing, terms, precision=lax.Precision.HIGH...  32.5 us
    reshape x1, local copies, waits for them, and re-layouts, local(): tile_transposed(part_values, sources).reshape(number, slots, tile, width_in)  19.2 us
    dot_general x1, local copies, waits for them, and re-layouts, tile_products(): jnp.einsum('kab,kbf->kaf', values, blocks, preferred_element_type=jnp.flo...  17.7 us
    dot_general x1, matrix products, tile_products(): jnp.einsum('kab,kbf->kaf', values, blocks, preferred_element_type=jnp.flo...  13.2 us
  transfers between devices with their start and end apart: 4, of which 2 were waited for; matrix products, arithmetic and copies ran while one was open for 23% of the time, Pallas kernels for 0%

commit v1 on v0

v1 whole, which is shorter than its diff:
```python
import functools

import jax
import jax.numpy as jnp
from jax import lax
from jax.experimental import pallas as pl
from jax.experimental.pallas import tpu as pltpu
from jax.sharding import PartitionSpec as P

MESH = pl.DeviceIdType.MESH
BF = jnp.bfloat16
F32 = jnp.float32
TILE = 128
WIDTH = 256
SECTIONS = 32
SLOTS = 4
QUARTER = 512
ROWS = 2048
VMEM_LIMIT = 50 << 20


class Place:
    def __init__(self):
        rows, rep = lax.axis_index("rows"), lax.axis_index("rep")
        self.yh, x, z = rows // 16, (rows // 4) % 4, rows % 4
        self.yl, self.core = rep // 2, rep % 2
        self.a = x + self.core * (z - x)
        self.b = z + self.core * (x - z)

    def section(self, yh, a, b):
        x = a + self.core * (b - a)
        z = b + self.core * (a - b)
        return yh * 16 + x * 4 + z

    def a_peer(self, j):
        return (self.section(self.yh, (self.a + j) % 4, self.b), self.yl * 2 + self.core)

    def b_peer(self, j):
        return (self.section(self.yh, self.a, (self.b + j) % 4), self.yl * 2 + self.core)

    def y_peer(self):
        return (self.section(1 - self.yh, self.a, self.b), self.yl * 2 + self.core)

    def near_peer(self, mask):
        yh = (self.yh + mask // 4) % 2
        yl = (self.yl + (mask // 2) % 2) % 2
        core = (self.core + mask % 2) % 2
        rows, _ = lax.axis_index("rows"), None
        return (yh * 16 + rows % 16, yl * 2 + core)

    def near_id(self):
        return self.yh * 4 + self.yl * 2 + self.core

    def chunk(self, b, a):
        return b * 4 + a + self.core * (a * 4 + b - b * 4 - a)


def greet(peers):
    barrier = pltpu.get_barrier_semaphore()
    for peer in peers:
        pl.semaphore_signal(barrier, inc=1, device_id=peer, device_id_type=MESH)
    pl.semaphore_wait(barrier, len(peers))


def remote(src, dst, send, recv, peer):
    return pltpu.make_async_remote_copy(
        src_ref=src, dst_ref=dst, send_sem=send, recv_sem=recv, device_id=peer, device_id_type=MESH
    )


def pull_kernel(
    features, pull_vec, pull_own, out, asked, *scratch
):
    dense, scratch = scratch[:8], scratch[8:]
    (packed, wants, own_sem, want_sem, ask_send, ask_recv,
     y_send, y_recv, a_send, a_recv, b_send, b_recv) = scratch
    me = Place()
    fetch = pltpu.make_async_copy(
        features.at[pl.ds((me.yl * 2 + me.core) * 4, 4)], dense[0], own_sem
    )
    fetch.start()
    greet([me.y_peer()] + [me.a_peer(j) for j in (1, 2, 3)] + [me.b_peer(j) for j in (1, 2, 3)])

    def ask(j):
        return remote(pull_vec, asked.at[j - 1], ask_send.at[j - 1], ask_recv.at[j - 1], me.b_peer(j))

    for j in (1, 2, 3):
        ask(j).start()
    fetch.wait()

    across = remote(dense[0], dense[4], y_send, y_recv, me.y_peer())

    def along(h, j):
        return remote(
            dense[4 * h], dense[4 * h + j], a_send.at[h, j - 1], a_recv.at[h, j - 1], me.a_peer(j)
        )

    def place(h, j):
        return (me.yh + h) % 2, (me.a + 4 - j) % 4

    def give(h, j, to):
        yh, a = place(h, j)
        n = 4 * h + j
        return remote(
            packed.at[to - 1, n], out.at[me.b * 8 + yh * 4 + a],
            b_send.at[to - 1, n], b_recv.at[to - 1, n], me.b_peer(to),
        )

    across.start()
    for j in (1, 3, 2):
        along(0, j).start()
    for j in (1, 2, 3):
        ask(j).wait()
        table = pltpu.make_async_copy(asked.at[j - 1], wants.at[j - 1], want_sem)
        table.start()
        table.wait()

    def serve(h, j):
        column = me.section(*place(h, j), me.b)
        for source in (1, 3, 2):
            to = 4 - source
            for p in range(2):
                packed[to - 1, 4 * h + j, p] = dense[4 * h + j][wants[source - 1, column, p]]
            give(h, j, to).start()

    serve(0, 0)
    across.wait()
    for j in (1, 3, 2):
        along(1, j).start()
    serve(1, 0)
    for h in range(2):
        for j in (1, 3, 2):
            along(h, j).wait_recv()
            serve(h, j)
    for h in range(2):
        for j in range(4):
            yh, a = place(h, j)
            column = me.section(yh, a, me.b)
            for p in range(2):
                out[me.b * 8 + yh * 4 + a, p] = dense[4 * h + j][pull_own[column, p]]
    for h in range(2):
        for j in (1, 2, 3):
            along(h, j).wait_send()
    for to in (1, 2, 3):
        for h in range(2):
            for j in range(4):
                give(h, j, to).wait()


def pull(features, pull_cols):
    dma = pltpu.SemaphoreType.DMA
    vmem = pl.BlockSpec(memory_space=pltpu.VMEM)
    return pl.pallas_call(
        pull_kernel,
        name="pull",
        out_shape=(
            jax.ShapeDtypeStruct((SECTIONS, 2, TILE, WIDTH), BF),
            jax.ShapeDtypeStruct((3, SECTIONS, 2), jnp.int32),
        ),
        in_specs=[pl.BlockSpec(memory_space=pl.ANY), vmem, pl.BlockSpec(memory_space=pltpu.SMEM)],
        out_specs=(vmem, vmem),
        scratch_shapes=[
            *[pltpu.VMEM((4, TILE, WIDTH), BF)] * 8,
            pltpu.VMEM((3, 8, 2, TILE, WIDTH), BF),
            pltpu.SMEM((3, SECTIONS, 2), jnp.int32),
            dma, dma, dma((3,)), dma((3,)),
            dma, dma, dma((2, 3)), dma((2, 3)), dma((3, 8)), dma((3, 8)),
        ],
        compiler_params=pltpu.CompilerParams(
            collective_id=1, has_side_effects=True, vmem_limit_bytes=VMEM_LIMIT
        ),
    )(features.reshape(16, TILE, WIDTH), pull_cols, pull_cols)


def masked(values, section, picks, counts):
    halves = []
    for p in range(2):
        parts = []
        for t in range(SLOTS):
            keep = jnp.logical_and(picks[section, t] == p, t < counts[0, section])
            scale = jnp.where(keep, jnp.float32(1), jnp.float32(0))
            parts.append(values[section, t] * jnp.full((TILE, TILE), scale, F32).astype(BF))
        halves.append(jnp.concatenate(parts, axis=0))
    return jnp.concatenate(halves, axis=1)


def forward_kernel(values, pulled, rows, picks, counts, total):
    me = Place()
    total[...] = jnp.zeros_like(total)

    def one(place, carry):
        section = me.section((place // 4) % 2, place % 4, place // 8)
        block = pulled[place].reshape(2 * TILE, WIDTH)
        terms = jnp.dot(masked(values, section, picks, counts), block, preferred_element_type=F32)
        for t in range(SLOTS):
            total[rows[section, t]] += terms[t * TILE:(t + 1) * TILE]
        return carry

    lax.fori_loop(0, SECTIONS, one, 0, unroll=2)


def forward(values, pulled, rows, picks, counts):
    vmem, smem = pl.BlockSpec(memory_space=pltpu.VMEM), pl.BlockSpec(memory_space=pltpu.SMEM)
    return pl.pallas_call(
        forward_kernel,
        name="forward",
        out_shape=jax.ShapeDtypeStruct((16, TILE, WIDTH), F32),
        in_specs=[vmem, vmem, smem, smem, smem],
        out_specs=vmem,
        compiler_params=pltpu.CompilerParams(vmem_limit_bytes=VMEM_LIMIT),
    )(values, pulled, rows, picks, counts)


def dense_kernel(
    part, weight, bias, cotangent, act, back, wpart,
    from_core, to_y, from_y, core_send, core_recv, y_send, y_recv,
    g_core_send, g_core_recv, g_y_send, g_y_recv, f_send, f_recv,
):
    me = Place()
    core_peer, y_peer = me.near_peer(1), me.near_peer(2)
    greet([core_peer, y_peer])
    quarters = [(1 - me.yl) * 2, me.yl * 2]

    def swap(n, t):
        src = part.at[(quarters[n] + 1 - me.core) * 4 + t]
        return remote(src, from_core.at[n, t], core_send.at[n, t], core_recv.at[n, t], core_peer)

    def over(t):
        return remote(to_y.at[t], from_y.at[t], y_send.at[t], y_recv.at[t], y_peer)

    for n in range(2):
        for t in range(4):
            swap(n, t).start()
    for t in range(4):
        swap(0, t).wait_recv()
        to_y[t] = (part[(quarters[0] + me.core) * 4 + t] + from_core[0, t]).astype(BF)
        over(t).start()

    mine = me.yl * 2 + me.core
    yours = (1 - me.yl) * 2 + me.core

    def share_core(t):
        ref = back.at[mine * 4 + t]
        return remote(ref, ref, g_core_send.at[t], g_core_recv.at[t], core_peer)

    def share_y(t):
        ref = back.at[mine * 4 + t]
        return remote(ref, ref, g_y_send.at[t], g_y_recv.at[t], y_peer)

    def forward_on(t):
        ref = back.at[yours * 4 + t]
        return remote(ref, ref, f_send.at[t], f_recv.at[t], core_peer)

    grad = jnp.zeros((WIDTH, WIDTH), F32)
    bias_sum = jnp.zeros((1, WIDTH), F32)
    for t in range(4):
        swap(1, t).wait_recv()
        over(t).wait_recv()
        agg = (part[mine * 4 + t] + from_core[1, t] + from_y[t].astype(F32)).astype(BF)
        pre = jnp.dot(agg, weight[...], preferred_element_type=F32) + bias[...]
        sig = 1.0 / (1.0 + jnp.exp(-pre))
        act[t] = (pre * sig).astype(BF)
        slope = (cotangent[t].astype(F32) * (sig * (1.0 + pre * (1.0 - sig)))).astype(BF)
        back[mine * 4 + t] = lax.dot_general(
            slope, weight[...], (((1,), (1,)), ((), ())), preferred_element_type=F32
        ).astype(BF)
        share_y(t).start()
        share_core(t).start()
        grad += lax.dot_general(agg, slope, (((0,), (0,)), ((), ())), preferred_element_type=F32)
        bias_sum += jnp.sum(slope.astype(F32), axis=0, keepdims=True)

    for t in range(4):
        share_y(t).wait_recv()
        forward_on(t).start()
    wpart[:, 16:24, :] = jnp.zeros((16, 8, WIDTH), F32)
    wpart[0, 16:17, :] = bias_sum
    wpart[:, :16, :] = grad.reshape(16, 16, WIDTH)
    for t in range(4):
        share_y(t).wait_send()
        share_core(t).wait()
        forward_on(t).wait()
        over(t).wait_send()
        for n in range(2):
            swap(n, t).wait_send()


def dense_layer(part, weight, bias, cotangent):
    dma = pltpu.SemaphoreType.DMA
    vmem = pl.BlockSpec(memory_space=pltpu.VMEM)
    return pl.pallas_call(
        dense_kernel,
        name="dense",
        out_shape=(
            jax.ShapeDtypeStruct((4, TILE, WIDTH), BF),
            jax.ShapeDtypeStruct((16, TILE, WIDTH), BF),
            jax.ShapeDtypeStruct((16, 24, WIDTH), F32),
        ),
        in_specs=[vmem] * 4,
        out_specs=(vmem,) * 3,
        scratch_shapes=[
            pltpu.VMEM((2, 4, TILE, WIDTH), F32),
            pltpu.VMEM((4, TILE, WIDTH), BF),
            pltpu.VMEM((4, TILE, WIDTH), BF),
            dma((2, 4)), dma((2, 4)), dma((4,)), dma((4,)),
            dma((4,)), dma((4,)), dma((4,)), dma((4,)), dma((4,)), dma((4,)),
        ],
        compiler_params=pltpu.CompilerParams(
            collective_id=2, has_side_effects=True, vmem_limit_bytes=VMEM_LIMIT
        ),
    )(part, weight, bias.reshape(1, WIDTH), cotangent.reshape(4, TILE, WIDTH))


def push_kernel(
    values, back, wpart, rows, picks, counts, pulls, asked,
    fgrad, wgrad, bgrad,
    terms, from_b, to_a, from_a, held, to_y, from_y,
    w0, w1, s1, w2, s2, w3, s4, w5,
    b_send, b_recv, a_send, a_recv, y_send, y_recv,
    w1_send, w1_recv, w2_send, w2_recv, w3_send, w3_recv, w4_send, w4_recv, w5_send, w5_recv,
):
    me = Place()
    greet(
        [me.near_peer(m) for m in range(1, 8)]
        + [me.a_peer(j) for j in (1, 2, 3)]
        + [me.b_peer(j) for j in (1, 2, 3)]
    )

    for b in range(4):
        for a in range(4):
            w0[b, a] = wpart[me.chunk(b, a)]

    def w1_copy(j):
        return remote(w0.at[(me.b + j) % 4], w1.at[j - 1], w1_send.at[j - 1], w1_recv.at[j - 1], me.b_peer(j))

    for j in (1, 2, 3):
        w1_copy(j).start()

    def place(k):
        return (me.yh + 1 + k) % 2, (me.a + 1 + k // 2) % 4

    def give(k, j):
        return remote(
            terms.at[j, k], from_b.at[j - 1, k], b_send.at[j - 1, k], b_recv.at[j - 1, k], me.b_peer(j)
        )

    def products(k, j):
        yh, a = place(k)
        section = me.section(yh, a, (me.b + j) % 4)
        sources = jnp.concatenate([back[rows[section, t]] for t in range(SLOTS)], axis=0)
        terms[j, k] = lax.dot_general(
            masked(values, section, picks, counts), sources, (((0,), (0,)), ((), ())),
            preferred_element_type=F32,
        ).astype(BF)

    def send_off(step, carry):
        k, j = step // 3, 1 + step % 3
        products(k, j)
        give(k, j).start()
        return carry

    lax.fori_loop(0, 24, send_off, 0)

    def keep(k, carry):
        products(k, 0)
        return carry

    lax.fori_loop(0, 8, keep, 0)

    def w2_copy(j):
        return remote(s1.at[(me.a + j) % 4], w2.at[j - 1], w2_send.at[j - 1], w2_recv.at[j - 1], me.a_peer(j))

    def w3_copy(m):
        return remote(s2, w3.at[me.near_id()], w3_send.at[m - 1], w3_recv.at[m - 1], me.near_peer(m))

    def w4_copy(j):
        return remote(s4.at[me.a], s4.at[me.a], w4_send.at[j - 1], w4_recv.at[j - 1], me.a_peer(j))

    def w5_copy(j):
        return remote(s4, w5.at[me.b], w5_send.at[j - 1], w5_recv.at[j - 1], me.b_peer(j))

    for j in (1, 2, 3):
        w1_copy(j).wait()
    s1[...] = w0[me.b] + w1[0] + w1[1] + w1[2]
    for j in (1, 2, 3):
        w2_copy(j).start()
    for j in (1, 2, 3):
        w2_copy(j).wait()
    s2[...] = s1[me.a] + w2[0] + w2[1] + w2[2]
    for m in range(1, 8):
        w3_copy(m).start()
    w3[me.near_id()] = s2[...]
    for m in range(1, 8):
        w3_copy(m).wait()
    total = w3[0]
    for m in range(1, 8):
        total = total + w3[m]
    s4[me.a] = total
    for j in (1, 2, 3):
        w4_copy(j).start()

    def along(k):
        j = 1 + k // 2
        return remote(to_a.at[k], from_a.at[k], a_send.at[k], a_recv.at[k], me.a_peer(j))

    def gather_b(k, q):
        yh, a = place(k)
        section = me.section(yh, a, me.b)
        sums = jnp.zeros((TILE, WIDTH), F32)
        for source in range(4):
            for p in range(2):
                if source == 0:
                    hit, tile = pulls[section, p] == q, terms[0, k, p * TILE:(p + 1) * TILE]
                else:
                    hit = asked[source - 1, section, p] == q
                    tile = from_b[source - 1, k, p * TILE:(p + 1) * TILE]
                sums += tile.astype(F32) * jnp.where(hit, jnp.float32(1), jnp.float32(0))
        return sums

    def first(k, carry):
        for j in (1, 2, 3):
            give(k, j).wait_recv()

        def column(q, inner):
            to_a[k, q] = gather_b(k, q).astype(BF)
            return inner

        lax.fori_loop(0, 4, column, 0)
        along(k).start()
        return carry

    lax.fori_loop(0, 6, first, 0)
    for k in (6, 7):
        for j in (1, 2, 3):
            give(k, j).wait_recv()

        def column(q, inner):
            held[k - 6, q] = gather_b(k, q)
            return inner

        lax.fori_loop(0, 4, column, 0)

    for j in (1, 2, 3):
        w4_copy(j).wait()
    for j in (1, 2, 3):
        w5_copy(j).start()
    w5[me.b] = s4[...]

    across = remote(to_y, from_y, y_send, y_recv, me.y_peer())
    for j in range(3):
        along(2 * j).wait_recv()
    for q in range(4):
        to_y[q] = (
            held[0, q] + from_a[0, q].astype(F32) + from_a[2, q].astype(F32) + from_a[4, q].astype(F32)
        ).astype(BF)
    across.start()
    for j in range(3):
        along(2 * j + 1).wait_recv()
    for q in range(4):
        held[1, q] = (
            held[1, q] + from_a[1, q].astype(F32) + from_a[3, q].astype(F32) + from_a[5, q].astype(F32)
        )
    for j in (1, 2, 3):
        w5_copy(j).wait()
    for b in range(4):
        for a in range(4):
            wgrad[me.chunk(b, a)] = w5[b, a, :16]
    bgrad[...] = w5[0, 0, 16:17]
    across.wait()
    for q in range(4):
        fgrad[q] = held[1, q] + from_y[q].astype(F32)

    def drain(step, carry):
        give(step // 3, 1 + step % 3).wait_send()
        return carry

    lax.fori_loop(0, 24, drain, 0)
    for k in range(6):
        along(k).wait_send()


def push(values, back, wpart, rows, picks, counts, pulls, asked):
    dma = pltpu.SemaphoreType.DMA
    vmem, smem = pl.BlockSpec(memory_space=pltpu.VMEM), pl.BlockSpec(memory_space=pltpu.SMEM)
    return pl.pallas_call(
        push_kernel,
        name="push",
        out_shape=(
            jax.ShapeDtypeStruct((4, TILE, WIDTH), F32),
            jax.ShapeDtypeStruct((16, 16, WIDTH), F32),
            jax.ShapeDtypeStruct((1, WIDTH), F32),
        ),
        in_specs=[vmem, vmem, vmem, smem, smem, smem, smem, smem],
        out_specs=(vmem,) * 3,
        scratch_shapes=[
            pltpu.VMEM((4, 8, 2 * TILE, WIDTH), BF),
            pltpu.VMEM((3, 8, 2 * TILE, WIDTH), BF),
            pltpu.VMEM((6, 4, TILE, WIDTH), BF),
            pltpu.VMEM((6, 4, TILE, WIDTH), BF),
            pltpu.VMEM((2, 4, TILE, WIDTH), F32),
            pltpu.VMEM((4, TILE, WIDTH), BF),
            pltpu.VMEM((4, TILE, WIDTH), BF),
            pltpu.VMEM((4, 4, 24, WIDTH), F32),
            pltpu.VMEM((3, 4, 24, WIDTH), F32),
            pltpu.VMEM((4, 24, WIDTH), F32),
            pltpu.VMEM((3, 24, WIDTH), F32),
            pltpu.VMEM((24, WIDTH), F32),
            pltpu.VMEM((8, 24, WIDTH), F32),
            pltpu.VMEM((4, 24, WIDTH), F32),
            pltpu.VMEM((4, 4, 24, WIDTH), F32),
            dma((3, 8)), dma((3, 8)), dma((6,)), dma((6,)), dma, dma,
            dma((3,)), dma((3,)), dma((3,)), dma((3,)), dma((7,)), dma((7,)),
            dma((3,)), dma((3,)), dma((3,)), dma((3,)),
        ],
        compiler_params=pltpu.CompilerParams(
            collective_id=3, has_side_effects=True, vmem_limit_bytes=VMEM_LIMIT
        ),
    )(values, back, wpart, rows, picks, counts, pulls, asked)


def local(
    features, weight, bias, cotangent, tile_vals, tile_rows, tile_pick, tile_count, pull_cols
):
    values = tile_vals.reshape(SECTIONS, SLOTS, TILE, TILE)
    rows = tile_rows.reshape(SECTIONS, SLOTS)
    picks = tile_pick.reshape(SECTIONS, SLOTS)
    counts = tile_count.reshape(1, SECTIONS)
    pulls = pull_cols.reshape(SECTIONS, 2)
    pulled, asked = pull(features, pulls)
    part = forward(values, pulled, rows, picks, counts)
    act, back, wpart = dense_layer(part, weight, bias, cotangent)
    fgrad, wgrad, bgrad = push(values, back, wpart, rows, picks, counts, pulls, asked)
    return (
        act.reshape(QUARTER, WIDTH),
        fgrad.reshape(QUARTER, WIDTH),
        wgrad.reshape(WIDTH, WIDTH),
        bgrad.reshape(WIDTH),
    )


def solution(mesh):
    in_specs = (
        P("rows", None),
        P(),
        P(),
        P(("rows", "rep"), None),
        P("rows", "rep", None, None, None, None),
        P("rows", "rep", None, None),
        P("rows", "rep", None, None),
        P("rows", "rep", None),
        P("rows", "rep", None, None),
    )
    out_specs = (P(("rows", "rep"), None), P(("rows", "rep"), None), P(), P())
    return jax.shard_map(local, mesh=mesh, in_specs=in_specs, out_specs=out_specs, check_vma=False)
```

time: 591 us -> 136 us (0.23)
  waiting for transfers between devices: 323 us -> 0 us
  Pallas kernels: 0 us -> 126 us
  blocking collectives: 106 us -> 0 us
  matrix products: 74.4 us -> 0 us
  local copies, waits for them, and re-layouts: 69.3 us -> 8.27 us
  between operations: 14 us -> 0.69 us
    reduce_scatter x1 -> x0, waiting for transfers between devices: 220 us -> none  [local(): lax.psum_scatter(placed.reshape(quarter * lax.axis_size('rows'), width_in...]
    pallas_call x0 -> x4, Pallas kernels: none -> 126 us  [the longest x1 52.9 us: push(): pl.pallas_call(push_kernel, name='push', out_shape=(jax.ShapeDtypeStruct(...]
    psum x2 -> x0, blocking collectives: 106 us -> none  [the longest x1 65.2 us: local(): weight_grad, bias_grad = lax.psum((weight_part, bias_part), ('rows', 'rep'))]
    all_gather x2 -> x0, waiting for transfers between devices: 103 us -> none  [the longest x1 103 us: local(): piece = lax.all_gather(own_quarter, 'rows', axis=0, tiled=True)]
    dot_general x7 -> x0, matrix products: 74.4 us -> none  [the longest x1 32.5 us: local(): jnp.einsum('stq,staf->sqaf', placing, terms, precision=lax.Precision.HIGH...]
    dot_general x3 -> x0, local copies, waits for them, and re-layouts: 25.6 us -> none  [the longest x1 17.7 us: tile_products(): jnp.einsum('kab,kbf->kaf', values, blocks, preferred_element_type=jnp.flo...]
    gather x7 -> x0, local copies, waits for them, and re-layouts: 18.5 us -> none  [the longest x1 10.1 us: local(): jnp.take(piece.reshape(number * col_tiles, tile, width_in), index, axis=0)]
    reshape x1 -> x3, local copies, waits for them, and re-layouts: 19.2 us -> 2.28 us  [the longest x1 0.76 us: local(): rows = tile_rows.reshape(SECTIONS, SLOTS)]
  transfers between devices with their start and end apart: 4 -> 0, of which waited for: 2 -> 0; matrix products, arithmetic and copies ran while one was open for 23% -> 0% of each run, Pallas kernels for 0% -> 0%
where the time goes in v1:
time: 136 us; the launch traced here: 135 us
  Pallas kernels  126 us (93%)
  local copies, waits for them, and re-layouts  8.27 us (6%)
    pallas_call x1, Pallas kernels, push(): pl.pallas_call(push_kernel, name='push', out_shape=(jax.ShapeDtypeStruct(...  52.9 us
    pallas_call x1, Pallas kernels, pull(): pl.pallas_call(pull_kernel, name='pull', out_shape=(jax.ShapeDtypeStruct(...  45.4 us
    pallas_call x1, Pallas kernels, dense_layer(): pl.pallas_call(dense_kernel, name='dense', out_shape=(jax.ShapeDtypeStruc...  18.7 us
    pallas_call x1, Pallas kernels, forward(): pl.pallas_call(forward_kernel, name='forward', out_shape=jax.ShapeDtypeSt...  9.24 us
    unnamed x16, local copies, waits for them, and re-layouts  5.99 us

profile of v1, /device:TPU:0, one launch (start us, length us, event | category | flops | bytes accessed | tf_op | source)
XLA Modules:
  0.0 135.1 jit_solution(15627998035425911309)
XLA Ops:
  0.6 0.8 copy.15.rows
  1.4 0.8 copy.16.picks
  2.2 0.8 copy.13.pull_vec.pull_own.pulls
  2.9 0.0 copy-start.1
  2.9 1.2 copy-done.1
  4.1 45.4 %pull.1 = (bf16[32,2,128,256]{3,2,1,0:T(8,128)(2,1)}, s32[3,32,2]{2,1,0:T(8,128)S(1)}) custom-call(bf16[16,128,256]{2,1,0:T(8,128)(2,1)S(1)} %bitcast.12, s32[32,2]{1,0:T(8,128)S(1)} %copy.13.pull_vec.pull_own.pulls, s32[32,2]{1,0:T(8,128)S(1)} %copy.13.pull_vec.pull_own.pulls), custom_call_target="tpu_custom_call" | custom-call | tf_op jit(solution)/shard_map/pull/pallas_call | solution.py:153
  49.5 0.0 copy-start.4
  49.5 0.6 copy-done.4
  50.2 0.0 copy-start.2
  50.2 0.0 copy-start.3
  50.2 0.0 copy-start.5
  50.2 9.2 %forward.1.part = f32[16,128,256]{2,1,0:T(8,128)S(1)} custom-call(bf16[32,4,128,128]{3,2,1,0:T(8,128)(2,1)} %bitcast.21, bf16[32,2,128,256]{3,2,1,0:T(8,128)(2,1)} %get-tuple-element.12.pulled, s32[32,4]{1,0:T(8,128)S(1)} %copy.15.rows, s32[32,4]{1,0:T(8,128)S(1)} %copy.16.picks, s32[1,32]{1,0:T(1,128)S(1)} %bitcast.17), custom_call_target="tpu_custom_call" | custom-call | tf_op jit(solution)/shard_map/forward/pallas_call | solution.py:204
  59.4 0.0 copy-start
  59.4 1.3 copy-done
  60.8 0.0 copy-done.2
  60.8 0.0 copy-done.3
  60.8 0.0 copy-done.5
  60.8 18.7 %dense.1 = (bf16[4,128,256]{2,1,0:T(8,128)(2,1)S(1)}, bf16[16,128,256]{2,1,0:T(8,128)(2,1)S(1)}, f32[16,24,256]{2,1,0:T(8,128)S(1)}) custom-call(f32[16,128,256]{2,1,0:T(8,128)} %copy-done, bf16[256,256]{1,0:T(8,128)(2,1)S(1)} %copy-done.3, f32[1,256]{1,0:T(1,128)S(1)} %bitcast.19, bf16[4,128,256]{2,1,0:T(8,128)(2,1)S(1)} %bitcast.14), custom_call_target="tpu_custom_call" | custom-call | tf_op jit(solution)/shard_map/dense/pallas_call | solution.py:290
  79.5 52.9 %push.1 = (f32[4,128,256]{2,1,0:T(8,128)S(1)}, f32[16,16,256]{2,1,0:T(8,128)S(1)}, f32[1,256]{1,0:T(1,128)S(1)}) custom-call(bf16[32,4,128,128]{3,2,1,0:T(8,128)(2,1)} %bitcast.22, bf16[16,128,256]{2,1,0:T(8,128)(2,1)S(1)} %get-tuple-element.14.back, f32[16,24,256]{2,1,0:T(8,128)S(1)} %get-tuple-element.15.wpart, s32[32,4]{1,0:T(8,128)S(1)} %copy.15.rows, ...), custom_call_target="tpu_custom_call" | custom-call | tf_op jit(solution)/shard_map/push/pallas_call | solution.py:484
  132.4 0.7 copy.24
  133.1 0.8 copy.25
  133.9 0.7 copy.26
  134.6 0.6 copy.27
Async XLA Ops:
  2.9 1.2 copy-start.1
  49.5 0.7 copy-start.4
  50.2 10.6 %copy-start.2 = (bf16[512,256]{1,0:T(8,128)(2,1)S(1)}, bf16[512,256]{1,0:T(8,128)(2,1)}, u32[]{:S(2)}) copy-start(bf16[512,256]{1,0:T(8,128)(2,1)} %param.12) | copy-start | bytes 786436
  50.2 10.6 %copy-start.3 = (bf16[256,256]{1,0:T(8,128)(2,1)S(1)}, bf16[256,256]{1,0:T(8,128)(2,1)}, u32[]{:S(2)}) copy-start(bf16[256,256]{1,0:T(8,128)(2,1)} %weight.1) | copy-start | bytes 393220
  50.2 10.6 %copy-start.5 = (f32[256]{0:T(256)S(1)}, f32[256]{0:T(256)}, u32[]{:S(2)}) copy-start(f32[256]{0:T(256)} %param.11) | copy-start | bytes 3076
  59.4 1.3 copy-start

commit v2 on v0

v2 whole, which is shorter than its diff:
```python
import functools

import jax
import jax.numpy as jnp
from jax import lax
from jax.experimental import pallas as pl
from jax.experimental.pallas import tpu as pltpu
from jax.sharding import PartitionSpec as P

MESH = pl.DeviceIdType.MESH
BF = jnp.bfloat16
F32 = jnp.float32
TILE = 128
WIDTH = 256
SECTIONS = 32
SLOTS = 4
QUARTER = 512
ROWS = 2048
VMEM_LIMIT = 60 << 20


class Place:
    def __init__(self):
        rows, rep = lax.axis_index("rows"), lax.axis_index("rep")
        self.yh, x, z = rows // 16, (rows // 4) % 4, rows % 4
        self.yl, self.core = rep // 2, rep % 2
        self.a = x + self.core * (z - x)
        self.b = z + self.core * (x - z)

    def section(self, yh, a, b):
        x = a + self.core * (b - a)
        z = b + self.core * (a - b)
        return yh * 16 + x * 4 + z

    def a_peer(self, j):
        return (self.section(self.yh, (self.a + j) % 4, self.b), self.yl * 2 + self.core)

    def b_peer(self, j):
        return (self.section(self.yh, self.a, (self.b + j) % 4), self.yl * 2 + self.core)

    def y_peer(self):
        return (self.section(1 - self.yh, self.a, self.b), self.yl * 2 + self.core)

    def near_peer(self, mask):
        yh = (self.yh + mask // 4) % 2
        yl = (self.yl + (mask // 2) % 2) % 2
        core = (self.core + mask % 2) % 2
        rows, _ = lax.axis_index("rows"), None
        return (yh * 16 + rows % 16, yl * 2 + core)

    def near_id(self):
        return self.yh * 4 + self.yl * 2 + self.core

    def chunk(self, b, a):
        return b * 4 + a + self.core * (a * 4 + b - b * 4 - a)


def greet(peers):
    barrier = pltpu.get_barrier_semaphore()
    for peer in peers:
        pl.semaphore_signal(barrier, inc=1, device_id=peer, device_id_type=MESH)
    pl.semaphore_wait(barrier, len(peers))


def remote(src, dst, send, recv, peer):
    return pltpu.make_async_remote_copy(
        src_ref=src, dst_ref=dst, send_sem=send, recv_sem=recv, device_id=peer, device_id_type=MESH
    )


def masked(values, section, picks, counts):
    halves = []
    for p in range(2):
        parts = []
        for t in range(SLOTS):
            keep = jnp.logical_and(picks[section, t] == p, t < counts[0, section])
            scale = jnp.where(keep, jnp.float32(1), jnp.float32(0))
            parts.append(values[section, t] * jnp.full((TILE, TILE), scale, F32).astype(BF))
        halves.append(jnp.concatenate(parts, axis=0))
    return jnp.concatenate(halves, axis=1)


def layer_kernel(
    features, values_hbm, weight, bias, cotangent, pull_vec, rows, picks, counts, pulls,
    act, fgrad, wgrad, bgrad, *scratch,
):
    dense, scratch = scratch[:8], scratch[8:]
    (values, asked, wants, packed, got, running, last,
     swap_out, from_core, to_near, from_near, back,
     terms, from_b, to_y, from_y, to_a, from_a, held,
     w0, w1, s1, w2, s2, w3, s4, w5,
     load_sem, own_sem, want_sem, ask_send, ask_recv,
     fa_send, fa_recv, fy_send, fy_recv, fb_send, fb_recv,
     core_send, core_recv, near_send, near_recv,
     gc_send, gc_recv, gn_send, gn_recv, gf_send, gf_recv,
     b_send, b_recv, y_send, y_recv, a_send, a_recv,
     w1_send, w1_recv, w2_send, w2_recv, w3_send, w3_recv, w4_send, w4_recv, w5_send, w5_recv) = scratch
    me = Place()
    fetch = pltpu.make_async_copy(
        features.at[pl.ds((me.yl * 2 + me.core) * 4, 4)], dense[0], own_sem
    )
    fetch.start()
    load = pltpu.make_async_copy(values_hbm, values, load_sem)
    load.start()
    greet(
        [me.near_peer(m) for m in range(1, 8)]
        + [me.a_peer(j) for j in (1, 2, 3)]
        + [me.b_peer(j) for j in (1, 2, 3)]
    )

    def ask(j):
        return remote(pull_vec, asked.at[j - 1], ask_send.at[j - 1], ask_recv.at[j - 1], me.b_peer(j))

    for j in (1, 2, 3):
        ask(j).start()
    fetch.wait()

    def along(j):
        return remote(dense[0], dense[j], fa_send.at[j - 1], fa_recv.at[j - 1], me.a_peer(j))

    def across(j):
        return remote(dense[j], dense[4 + j], fy_send.at[j], fy_recv.at[j], me.y_peer())

    def give(n, to):
        return remote(
            packed.at[to - 1, n], got.at[to, n], fb_send.at[to - 1, n], fb_recv.at[to - 1, n], me.b_peer(to)
        )

    def block_section(n, b):
        return me.section((me.yh + n // 4) % 2, (me.a + 4 - n % 4) % 4, b)

    for j in (1, 3, 2):
        along(j).start()
    across(0).start()
    for j in (1, 2, 3):
        ask(j).wait()
        table = pltpu.make_async_copy(asked.at[j - 1], wants.at[j - 1], want_sem)
        table.start()
        table.wait()

    def serve(n):
        column = block_section(n, me.b)
        for source in (1, 3, 2):
            to = 4 - source
            for p in range(2):
                packed[to - 1, n, p] = dense[n][wants[source - 1, column, p]]
            give(n, to).start()
        for p in range(2):
            got[0, n, p] = dense[n][pulls[column, p]]

    serve(0)
    for j in (1, 3, 2):
        along(j).wait_recv()
        across(j).start()
        serve(j)
    for j in (0, 1, 3, 2):
        across(j).wait_recv()
        serve(4 + j)

    load.wait()
    running[128] = jnp.zeros((TILE, WIDTH), F32)

    def forward(step, carry):
        ends = list(carry)
        n = step // 4 * 4 + (step % 4 + (step % 4) // 2 * (5 - 2 * (step % 4)))
        for j in (1, 2, 3):
            give(n, j).wait_recv()
        for source in range(4):
            section = block_section(n, (me.b + 4 - source) % 4)
            block = got[source, n].reshape(2 * TILE, WIDTH)
            sums = jnp.dot(masked(values, section, picks, counts), block, preferred_element_type=F32)
            for t in range(SLOTS):
                row = rows[section, t]
                before = jnp.int32(128)
                slot = (step * 4 + source) * 4 + t
                for r in range(16):
                    before = jnp.where(row == r, ends[r], before)
                    ends[r] = jnp.where(row == r, slot, ends[r])
                running[slot] = sums[t * TILE:(t + 1) * TILE] + running[before]
        return tuple(ends)

    ends = lax.fori_loop(0, 8, forward, (jnp.int32(128),) * 16)
    for r in range(16):
        last[r] = ends[r]

    def part(r):
        return running[last[r]]

    core_peer, near_peer = me.near_peer(1), me.near_peer(2)
    quarters = [(1 - me.yl) * 2, me.yl * 2]

    def swap(n, t):
        return remote(swap_out.at[n, t], from_core.at[n, t], core_send.at[n, t], core_recv.at[n, t], core_peer)

    def over(t):
        return remote(to_near.at[t], from_near.at[t], near_send.at[t], near_recv.at[t], near_peer)

    for n in range(2):
        for t in range(4):
            swap_out[n, t] = part((quarters[n] + 1 - me.core) * 4 + t)
            swap(n, t).start()
    for t in range(4):
        swap(0, t).wait_recv()
        to_near[t] = (part((quarters[0] + me.core) * 4 + t) + from_core[0, t]).astype(BF)
        over(t).start()

    mine = me.yl * 2 + me.core
    yours = (1 - me.yl) * 2 + me.core

    def share_core(t):
        ref = back.at[mine * 4 + t]
        return remote(ref, ref, gc_send.at[t], gc_recv.at[t], core_peer)

    def share_near(t):
        ref = back.at[mine * 4 + t]
        return remote(ref, ref, gn_send.at[t], gn_recv.at[t], near_peer)

    def forward_on(t):
        ref = back.at[yours * 4 + t]
        return remote(ref, ref, gf_send.at[t], gf_recv.at[t], core_peer)

    grad = jnp.zeros((WIDTH, WIDTH), F32)
    bias_sum = jnp.zeros((1, WIDTH), F32)
    for t in range(4):
        swap(1, t).wait_recv()
        over(t).wait_recv()
        agg = (part(mine * 4 + t) + from_core[1, t] + from_near[t].astype(F32)).astype(BF)
        pre = jnp.dot(agg, weight[...], preferred_element_type=F32) + bias[...]
        sig = 1.0 / (1.0 + jnp.exp(-pre))
        act[t] = (pre * sig).astype(BF)
        slope = (cotangent[t].astype(F32) * (sig * (1.0 + pre * (1.0 - sig)))).astype(BF)
        back[mine * 4 + t] = lax.dot_general(
            slope, weight[...], (((1,), (1,)), ((), ())), preferred_element_type=F32
        ).astype(BF)
        share_near(t).start()
        share_core(t).start()
        grad += lax.dot_general(agg, slope, (((0,), (0,)), ((), ())), preferred_element_type=F32)
        bias_sum += jnp.sum(slope.astype(F32), axis=0, keepdims=True)

    for c in range(16):
        b, a = c // 4, c % 4
        w0[b + me.core * (a - b), a + me.core * (b - a), :16] = grad[c * 16:(c + 1) * 16]
        w0[b, a, 16:24] = jnp.zeros((8, WIDTH), F32)
    w0[0, 0, 16:17] = bias_sum

    def w1_copy(j):
        return remote(w0.at[(me.b + j) % 4], w1.at[j - 1], w1_send.at[j - 1], w1_recv.at[j - 1], me.b_peer(j))

    def w2_copy(j):
        return remote(s1.at[(me.a + j) % 4], w2.at[j - 1], w2_send.at[j - 1], w2_recv.at[j - 1], me.a_peer(j))

    def w3_copy(m):
        return remote(s2, w3.at[me.near_id()], w3_send.at[m - 1], w3_recv.at[m - 1], me.near_peer(m))

    def w4_copy(j):
        return remote(s4.at[me.a], s4.at[me.a], w4_send.at[j - 1], w4_recv.at[j - 1], me.a_peer(j))

    def w5_copy(j):
        return remote(s4, w5.at[me.b], w5_send.at[j - 1], w5_recv.at[j - 1], me.b_peer(j))

    for j in (1, 2, 3):
        w1_copy(j).start()

    for t in range(4):
        share_near(t).wait_recv()
        forward_on(t).start()
    for t in range(4):
        share_core(t).wait()
        forward_on(t).wait()

    def place(k):
        return (me.yh + 1 + k // 4) % 2, (me.a + 1 + k % 4) % 4

    def send_b(k, j):
        return remote(
            terms.at[j, k], from_b.at[j - 1, k], b_send.at[j - 1, k], b_recv.at[j - 1, k], me.b_peer(j)
        )

    def products(k, j):
        yh, a = place(k)
        section = me.section(yh, a, (me.b + j) % 4)
        sources = jnp.concatenate([back[rows[section, t]] for t in range(SLOTS)], axis=0)
        terms[j, k] = lax.dot_general(
            masked(values, section, picks, counts), sources, (((0,), (0,)), ((), ())),
            preferred_element_type=F32,
        ).astype(BF)

    def contribute(k, carry):
        for j in (1, 3, 2):
            products(k, j)
            send_b(k, j).start()
        return carry

    def keep(k, carry):
        products(k, 0)
        return carry

    lax.fori_loop(0, 8, contribute, 0)
    lax.fori_loop(0, 8, keep, 0)

    def send_y(k):
        return remote(to_y.at[k], from_y.at[k], y_send.at[k], y_recv.at[k], me.y_peer())

    def send_a(k):
        return remote(to_a.at[k], from_a.at[k], a_send.at[k], a_recv.at[k], me.a_peer(1 + k))

    def gather_b(k, q):
        yh, a = place(k)
        section = me.section(yh, a, me.b)
        sums = jnp.zeros((TILE, WIDTH), F32)
        for source in range(4):
            for p in range(2):
                if source == 0:
                    hit, tile = pulls[section, p] == q, terms[0, k, p * TILE:(p + 1) * TILE]
                else:
                    hit = wants[source - 1, section, p] == q
                    tile = from_b[source - 1, k, p * TILE:(p + 1) * TILE]
                sums += tile.astype(F32) * jnp.where(hit, jnp.float32(1), jnp.float32(0))
        return sums

    def arrive_b(k):
        for j in (1, 2, 3):
            send_b(k, j).wait_recv()

    def other_half(k):
        arrive_b(k)

        def column(q, inner):
            to_y[k, q] = gather_b(k, q).astype(BF)
            return inner

        lax.fori_loop(0, 4, column, 0)
        send_y(k).start()

    def this_half(k):
        arrive_b(4 + k)
        send_y(k).wait_recv()

        def column(q, inner):
            sums = gather_b(4 + k, q) + from_y[k, q].astype(F32)
            if k < 3:
                to_a[k, q] = sums.astype(BF)
            else:
                held[q] = sums
            return inner

        lax.fori_loop(0, 4, column, 0)
        if k < 3:
            send_a(k).start()

    other_half(0)
    for j in (1, 2, 3):
        w1_copy(j).wait()
    s1[...] = w0[me.b] + w1[0] + w1[1] + w1[2]
    for j in (1, 2, 3):
        w2_copy(j).start()
    other_half(1)
    other_half(2)
    for j in (1, 2, 3):
        w2_copy(j).wait()
    s2[...] = s1[me.a] + w2[0] + w2[1] + w2[2]
    for m in range(1, 8):
        w3_copy(m).start()
    w3[me.near_id()] = s2[...]
    other_half(3)
    this_half(0)
    for m in range(1, 8):
        w3_copy(m).wait()
    total = w3[0]
    for m in range(1, 8):
        total = total + w3[m]
    s4[me.a] = total
    for j in (1, 2, 3):
        w4_copy(j).start()
    this_half(1)
    this_half(2)
    for j in (1, 2, 3):
        w4_copy(j).wait()
    for j in (1, 2, 3):
        w5_copy(j).start()
    w5[me.b] = s4[...]
    this_half(3)
    for j in (1, 2, 3):
        w5_copy(j).wait()
    for b in range(4):
        for a in range(4):
            wgrad[me.chunk(b, a)] = w5[b, a, :16]
    bgrad[...] = w5[0, 0, 16:17]
    for k in range(3):
        send_a(k).wait_recv()
    for q in range(4):
        fgrad[q] = held[q] + from_a[0, q].astype(F32) + from_a[1, q].astype(F32) + from_a[2, q].astype(F32)

    for j in (1, 2, 3):
        along(j).wait_send()
    for j in range(4):
        across(j).wait_send()
        over(j).wait_send()
        share_near(j).wait_send()
        send_y(j).wait_send()
        for n in range(2):
            swap(n, j).wait_send()
    for k in range(3):
        send_a(k).wait_send()

    def drain(n, carry):
        for j in (1, 2, 3):
            give(n, j).wait_send()
            send_b(n, j).wait_send()
        return carry

    lax.fori_loop(0, 8, drain, 0)


def layer(features, values, weight, bias, cotangent, rows, picks, counts, pulls):
    dma = pltpu.SemaphoreType.DMA
    vmem, smem = pl.BlockSpec(memory_space=pltpu.VMEM), pl.BlockSpec(memory_space=pltpu.SMEM)
    hbm = pl.BlockSpec(memory_space=pl.ANY)
    return pl.pallas_call(
        layer_kernel,
        name="layer",
        out_shape=(
            jax.ShapeDtypeStruct((4, TILE, WIDTH), BF),
            jax.ShapeDtypeStruct((4, TILE, WIDTH), F32),
            jax.ShapeDtypeStruct((16, 16, WIDTH), F32),
            jax.ShapeDtypeStruct((1, WIDTH), F32),
        ),
        in_specs=[hbm, hbm, vmem, vmem, vmem, vmem, smem, smem, smem, smem],
        out_specs=(vmem,) * 4,
        scratch_shapes=[
            *[pltpu.VMEM((4, TILE, WIDTH), BF)] * 8,
            pltpu.VMEM((SECTIONS, SLOTS, TILE, TILE), BF),
            pltpu.VMEM((3, SECTIONS, 2), jnp.int32),
            pltpu.SMEM((3, SECTIONS, 2), jnp.int32),
            pltpu.VMEM((3, 8, 2, TILE, WIDTH), BF),
            pltpu.VMEM((4, 8, 2, TILE, WIDTH), BF),
            pltpu.VMEM((129, TILE, WIDTH), F32),
            pltpu.SMEM((16,), jnp.int32),
            pltpu.VMEM((2, 4, TILE, WIDTH), F32),
            pltpu.VMEM((2, 4, TILE, WIDTH), F32),
            pltpu.VMEM((4, TILE, WIDTH), BF),
            pltpu.VMEM((4, TILE, WIDTH), BF),
            pltpu.VMEM((16, TILE, WIDTH), BF),
            pltpu.VMEM((4, 8, 2 * TILE, WIDTH), BF),
            pltpu.VMEM((3, 8, 2 * TILE, WIDTH), BF),
            pltpu.VMEM((4, 4, TILE, WIDTH), BF),
            pltpu.VMEM((4, 4, TILE, WIDTH), BF),
            pltpu.VMEM((3, 4, TILE, WIDTH), BF),
            pltpu.VMEM((3, 4, TILE, WIDTH), BF),
            pltpu.VMEM((4, TILE, WIDTH), F32),
            pltpu.VMEM((4, 4, 24, WIDTH), F32),
            pltpu.VMEM((3, 4, 24, WIDTH), F32),
            pltpu.VMEM((4, 24, WIDTH), F32),
            pltpu.VMEM((3, 24, WIDTH), F32),
            pltpu.VMEM((24, WIDTH), F32),
            pltpu.VMEM((8, 24, WIDTH), F32),
            pltpu.VMEM((4, 24, WIDTH), F32),
            pltpu.VMEM((4, 4, 24, WIDTH), F32),
            dma, dma, dma, dma((3,)), dma((3,)),
            dma((3,)), dma((3,)), dma((4,)), dma((4,)), dma((3, 8)), dma((3, 8)),
            dma((2, 4)), dma((2, 4)), dma((4,)), dma((4,)),
            dma((4,)), dma((4,)), dma((4,)), dma((4,)), dma((4,)), dma((4,)),
            dma((3, 8)), dma((3, 8)), dma((4,)), dma((4,)), dma((3,)), dma((3,)),
            dma((3,)), dma((3,)), dma((3,)), dma((3,)), dma((7,)), dma((7,)),
            dma((3,)), dma((3,)), dma((3,)), dma((3,)),
        ],
        compiler_params=pltpu.CompilerParams(
            collective_id=1, has_side_effects=True, vmem_limit_bytes=VMEM_LIMIT
        ),
    )(
        features.reshape(16, TILE, WIDTH), values, weight, bias.reshape(1, WIDTH),
        cotangent.reshape(4, TILE, WIDTH), pulls, rows, picks, counts, pulls,
    )


def local(
    features, weight, bias, cotangent, tile_vals, tile_rows, tile_pick, tile_count, pull_cols
):
    act, fgrad, wgrad, bgrad = layer(
        features,
        tile_vals.reshape(SECTIONS, SLOTS, TILE, TILE),
        weight,
        bias,
        cotangent,
        tile_rows.reshape(SECTIONS, SLOTS),
        tile_pick.reshape(SECTIONS, SLOTS),
        tile_count.reshape(1, SECTIONS),
        pull_cols.reshape(SECTIONS, 2),
    )
    return (
        act.reshape(QUARTER, WIDTH),
        fgrad.reshape(QUARTER, WIDTH),
        wgrad.reshape(WIDTH, WIDTH),
        bgrad.reshape(WIDTH),
    )


def solution(mesh):
    in_specs = (
        P("rows", None),
        P(),
        P(),
        P(("rows", "rep"), None),
        P("rows", "rep", None, None, None, None),
        P("rows", "rep", None, None),
        P("rows", "rep", None, None),
        P("rows", "rep", None),
        P("rows", "rep", None, None),
    )
    out_specs = (P(("rows", "rep"), None), P(("rows", "rep"), None), P(), P())
    return jax.shard_map(local, mesh=mesh, in_specs=in_specs, out_specs=out_specs, check_vma=False)
```

time: 591 us -> 114 us (0.19)
  waiting for transfers between devices: 323 us -> 0 us
  blocking collectives: 106 us -> 0 us
  Pallas kernels: 0 us -> 103 us
  matrix products: 74.4 us -> 0 us
  local copies, waits for them, and re-layouts: 69.3 us -> 10.5 us
  between operations: 14 us -> 0.64 us
    reduce_scatter x1 -> x0, waiting for transfers between devices: 220 us -> none  [local(): lax.psum_scatter(placed.reshape(quarter * lax.axis_size('rows'), width_in...]
    psum x2 -> x0, blocking collectives: 106 us -> none  [the longest x1 65.2 us: local(): weight_grad, bias_grad = lax.psum((weight_part, bias_part), ('rows', 'rep'))]
    all_gather x2 -> x0, waiting for transfers between devices: 103 us -> none  [the longest x1 103 us: local(): piece = lax.all_gather(own_quarter, 'rows', axis=0, tiled=True)]
    pallas_call x0 -> x1, Pallas kernels: none -> 103 us  [layer(): pl.pallas_call(layer_kernel, name='layer', out_shape=(jax.ShapeDtypeStruc...]
    dot_general x7 -> x0, matrix products: 74.4 us -> none  [the longest x1 32.5 us: local(): jnp.einsum('stq,staf->sqaf', placing, terms, precision=lax.Precision.HIGH...]
    dot_general x3 -> x0, local copies, waits for them, and re-layouts: 25.6 us -> none  [the longest x1 17.7 us: tile_products(): jnp.einsum('kab,kbf->kaf', values, blocks, preferred_element_type=jnp.flo...]
    gather x7 -> x0, local copies, waits for them, and re-layouts: 18.5 us -> none  [the longest x1 10.1 us: local(): jnp.take(piece.reshape(number * col_tiles, tile, width_in), index, axis=0)]
    reshape x1 -> x3, local copies, waits for them, and re-layouts: 19.2 us -> 4.1 us  [the longest x1 1.37 us: local(): tile_rows.reshape(SECTIONS, SLOTS)]
  transfers between devices with their start and end apart: 4 -> 0, of which waited for: 2 -> 0; matrix products, arithmetic and copies ran while one was open for 23% -> 0% of each run, Pallas kernels for 0% -> 0%
where the time goes in v2:
time: 114 us
  Pallas kernels  103 us (90%)
  local copies, waits for them, and re-layouts  10.5 us (9%)
    pallas_call x1, Pallas kernels, layer(): pl.pallas_call(layer_kernel, name='layer', out_shape=(jax.ShapeDtypeStruc...  103 us
    unnamed x4, local copies, waits for them, and re-layouts  6.45 us

profile of v2, /device:TPU:0, one launch (start us, length us, event | category | flops | bytes accessed | tf_op | source)
XLA Modules:
  0.0 113.7 jit_solution(677816472480302295)
XLA Ops:
  0.6 1.4 %copy.14.rows = s32[32,4]{1,0:T(8,128)} copy(s32[32,4]{0,1:T(4,128)} %bitcast.18) | data formatting | bytes 1024 | tf_op jit(solution)/shard_map/reshape | solution.py:485
  2.0 1.4 %copy.15.picks = s32[32,4]{1,0:T(8,128)} copy(s32[32,4]{0,1:T(4,128)} %bitcast.19) | data formatting | bytes 1024 | tf_op jit(solution)/shard_map/reshape | solution.py:486
  3.4 1.4 %copy.13.pull_vec.pulls = s32[32,2]{1,0:T(8,128)} copy(s32[32,2]{0,1:T(2,128)} %bitcast.21) | data formatting | bytes 512 | tf_op jit(solution)/shard_map/reshape | solution.py:488
  4.7 102.5 %layer.1 = (bf16[4,128,256]{2,1,0:T(8,128)(2,1)}, f32[4,128,256]{2,1,0:T(8,128)}, f32[16,16,256]{2,1,0:T(8,128)}, f32[1,256]{1,0:T(1,128)}) custom-call(bf16[16,128,256]{2,1,0:T(8,128)(2,1)} %bitcast.13, bf16[32,4,128,128]{3,2,1,0:T(8,128)(2,1)} %bitcast.12, bf16[256,256]{1,0:T(8,128)(2,1)} %weight.1, f32[1,256]{1,0:T(1,128)} %bitcast.20, ...), custom_call_target="tpu_custom_call" | custom-call | tf_op jit(solution)/shard_map/layer/pallas_call | solution.py:419
  107.2 1.7 %copy.21 = bf16[512,256]{1,0:T(8,128)(2,1)} copy(bf16[512,256]{1,0:T(8,128)(2,1)} %bitcast.17) | data formatting | bytes 524288
  108.9 1.9 %copy.22 = f32[512,256]{1,0:T(8,128)} copy(f32[512,256]{1,0:T(8,128)} %bitcast.14) | data formatting | bytes 1048576
  110.8 1.7 %copy.23 = f32[256,256]{1,0:T(8,128)} copy(f32[256,256]{1,0:T(8,128)} %bitcast.16) | data formatting | bytes 524288
  112.4 1.2 %copy.24 = f32[256]{0:T(256)} copy(f32[256]{0:T(256)} %bitcast.22) | data formatting | bytes 2048

commit v3 on v2

--- a/solution.py
+++ b/solution.py
@@ -23,6 +23,7 @@
     def __init__(self):
         rows, rep = lax.axis_index("rows"), lax.axis_index("rep")
         self.yh, x, z = rows // 16, (rows // 4) % 4, rows % 4
+        self.x, self.z = x, z
         self.yl, self.core = rep // 2, rep % 2
         self.a = x + self.core * (z - x)
         self.b = z + self.core * (x - z)
@@ -45,14 +46,19 @@
         yh = (self.yh + mask // 4) % 2
         yl = (self.yl + (mask // 2) % 2) % 2
         core = (self.core + mask % 2) % 2
-        rows, _ = lax.axis_index("rows"), None
+        rows = lax.axis_index("rows")
         return (yh * 16 + rows % 16, yl * 2 + core)
 
     def near_id(self):
         return self.yh * 4 + self.yl * 2 + self.core
 
-    def chunk(self, b, a):
-        return b * 4 + a + self.core * (a * 4 + b - b * 4 - a)
+    def x_peer(self, j):
+        rows = lax.axis_index("rows")
+        return (self.yh * 16 + (rows + 4 * j) % 16, self.yl * 2 + self.core)
+
+    def z_peer(self, j):
+        rows = lax.axis_index("rows")
+        return (rows // 4 * 4 + (rows + j) % 4, self.yl * 2 + self.core)
 
 
 def greet(peers):
@@ -73,7 +79,7 @@
     for p in range(2):
         parts = []
         for t in range(SLOTS):
-            keep = jnp.logical_and(picks[section, t] == p, t < counts[0, section])
+            keep = jnp.logical_and(picks[t, section] == p, t < counts[0, section])
             scale = jnp.where(keep, jnp.float32(1), jnp.float32(0))
             parts.append(values[section, t] * jnp.full((TILE, TILE), scale, F32).astype(BF))
         halves.append(jnp.concatenate(parts, axis=0))
@@ -81,27 +87,33 @@
 
 
 def layer_kernel(
-    features, values_hbm, weight, bias, cotangent, pull_vec, rows, picks, counts, pulls,
-    act, fgrad, wgrad, bgrad, *scratch,
+    features, values_hbm, weight_hbm, bias, cot_hbm, pull_vec, rows, picks, counts, pulls,
+    act_out, fgrad_out, wgrad_out, bgrad, *scratch,
 ):
     dense, scratch = scratch[:8], scratch[8:]
-    (values, asked, wants, packed, got, running, last,
-     swap_out, from_core, to_near, from_near, back,
-     terms, from_b, to_y, from_y, to_a, from_a, held,
-     w0, w1, s1, w2, s2, w3, s4, w5,
-     load_sem, own_sem, want_sem, ask_send, ask_recv,
+    (values, weight, cotangent, asked, wants, packed, got, running, last,
+     swap_out, from_core, to_near, from_near, agg_all, slope_all, act, back,
+     terms, from_b, to_y, from_y, to_a, from_a, held, fgrad,
+     w0, n1, s1, w2, s2, w3, s4, wgrad, b1, x1, b2, z1,
+     load_sem, weight_sem, cot_sem, own_sem, want_sem, act_sem, fgrad_sem, wgrad_sem, ask_send, ask_recv,
      fa_send, fa_recv, fy_send, fy_recv, fb_send, fb_recv,
      core_send, core_recv, near_send, near_recv,
      gc_send, gc_recv, gn_send, gn_recv, gf_send, gf_recv,
      b_send, b_recv, y_send, y_recv, a_send, a_recv,
-     w1_send, w1_recv, w2_send, w2_recv, w3_send, w3_recv, w4_send, w4_recv, w5_send, w5_recv) = scratch
+     n1_send, n1_recv, w2_send, w2_recv, w3_send, w3_recv, w4_send, w4_recv, w5_send, w5_recv,
+     x1_send, x1_recv, z1_send, z1_recv) = scratch
     me = Place()
     fetch = pltpu.make_async_copy(
         features.at[pl.ds((me.yl * 2 + me.core) * 4, 4)], dense[0], own_sem
     )
     fetch.start()
-    load = pltpu.make_async_copy(values_hbm, values, load_sem)
-    load.start()
+    loads = [
+        pltpu.make_async_copy(values_hbm, values, load_sem),
+        pltpu.make_async_copy(weight_hbm, weight, weight_sem),
+        pltpu.make_async_copy(cot_hbm, cotangent, cot_sem),
+    ]
+    for load in loads:
+        load.start()
     greet(
         [me.near_peer(m) for m in range(1, 8)]
         + [me.a_peer(j) for j in (1, 2, 3)]
@@ -143,10 +155,10 @@
         for source in (1, 3, 2):
             to = 4 - source
             for p in range(2):
-                packed[to - 1, n, p] = dense[n][wants[source - 1, column, p]]
+                packed[to - 1, n, p] = dense[n][wants[source - 1, p, column]]
             give(n, to).start()
         for p in range(2):
-            got[0, n, p] = dense[n][pulls[column, p]]
+            got[0, n, p] = dense[n][pulls[p, column]]
 
     serve(0)
     for j in (1, 3, 2):
@@ -157,7 +169,8 @@
         across(j).wait_recv()
         serve(4 + j)
 
-    load.wait()
+    for load in loads:
+        load.wait()
     running[128] = jnp.zeros((TILE, WIDTH), F32)
 
     def forward(step, carry):
@@ -170,7 +183,7 @@
             block = got[source, n].reshape(2 * TILE, WIDTH)
             sums = jnp.dot(masked(values, section, picks, counts), block, preferred_element_type=F32)
             for t in range(SLOTS):
-                row = rows[section, t]
+                row = rows[t, section]
                 before = jnp.int32(128)
                 slot = (step * 4 + source) * 4 + t
                 for r in range(16):
@@ -219,47 +232,105 @@
         ref = back.at[yours * 4 + t]
         return remote(ref, ref, gf_send.at[t], gf_recv.at[t], core_peer)
 
-    grad = jnp.zeros((WIDTH, WIDTH), F32)
-    bias_sum = jnp.zeros((1, WIDTH), F32)
     for t in range(4):
         swap(1, t).wait_recv()
         over(t).wait_recv()
         agg = (part(mine * 4 + t) + from_core[1, t] + from_near[t].astype(F32)).astype(BF)
+        agg_all[t * TILE:(t + 1) * TILE] = agg
         pre = jnp.dot(agg, weight[...], preferred_element_type=F32) + bias[...]
         sig = 1.0 / (1.0 + jnp.exp(-pre))
         act[t] = (pre * sig).astype(BF)
         slope = (cotangent[t].astype(F32) * (sig * (1.0 + pre * (1.0 - sig)))).astype(BF)
+        slope_all[t * TILE:(t + 1) * TILE] = slope
         back[mine * 4 + t] = lax.dot_general(
             slope, weight[...], (((1,), (1,)), ((), ())), preferred_element_type=F32
         ).astype(BF)
         share_near(t).start()
         share_core(t).start()
-        grad += lax.dot_general(agg, slope, (((0,), (0,)), ((), ())), preferred_element_type=F32)
-        bias_sum += jnp.sum(slope.astype(F32), axis=0, keepdims=True)
-
-    for c in range(16):
-        b, a = c // 4, c % 4
-        w0[b + me.core * (a - b), a + me.core * (b - a), :16] = grad[c * 16:(c + 1) * 16]
-        w0[b, a, 16:24] = jnp.zeros((8, WIDTH), F32)
-    w0[0, 0, 16:17] = bias_sum
-
-    def w1_copy(j):
-        return remote(w0.at[(me.b + j) % 4], w1.at[j - 1], w1_send.at[j - 1], w1_recv.at[j - 1], me.b_peer(j))
+    give_act = pltpu.make_async_copy(act, act_out, act_sem)
+    give_act.start()
+
+    grad = lax.dot_general(
+        agg_all[...], slope_all[...], (((0,), (0,)), ((), ())), preferred_element_type=F32
+    )
+    bias_sum = jnp.sum(slope_all[...].astype(F32), axis=0, keepdims=True)
+    for m in range(8):
+        w0[m, :32] = grad[m * 32:(m + 1) * 32]
+        w0[m, 32:40] = jnp.broadcast_to(bias_sum, (8, WIDTH))
+
+    def n1_copy(m):
+        other = (me.yh + m // 4) % 2 * 4 + (me.yl + m // 2 % 2) % 2 * 2 + (me.core + m % 2) % 2
+        return remote(
+            w0.at[other], n1.at[me.near_id()], n1_send.at[m - 1], n1_recv.at[m - 1], me.near_peer(m)
+        )
 
     def w2_copy(j):
-        return remote(s1.at[(me.a + j) % 4], w2.at[j - 1], w2_send.at[j - 1], w2_recv.at[j - 1], me.a_peer(j))
-
-    def w3_copy(m):
-        return remote(s2, w3.at[me.near_id()], w3_send.at[m - 1], w3_recv.at[m - 1], me.near_peer(m))
+        return remote(
+            s1.at[(me.a + j) % 4], w2.at[me.a], w2_send.at[j - 1], w2_recv.at[j - 1], me.a_peer(j)
+        )
+
+    def x1_copy(j):
+        return remote(b1, x1.at[me.x], x1_send.at[j - 1], x1_recv.at[j - 1], me.x_peer(j))
+
+    def w3_copy(j):
+        return remote(s2, w3.at[me.b], w3_send.at[j - 1], w3_recv.at[j - 1], me.b_peer(j))
+
+    def z1_copy(j):
+        return remote(b2, z1.at[me.z], z1_send.at[j - 1], z1_recv.at[j - 1], me.z_peer(j))
 
     def w4_copy(j):
         return remote(s4.at[me.a], s4.at[me.a], w4_send.at[j - 1], w4_recv.at[j - 1], me.a_peer(j))
 
-    def w5_copy(j):
-        return remote(s4, w5.at[me.b], w5_send.at[j - 1], w5_recv.at[j - 1], me.b_peer(j))
-
-    for j in (1, 2, 3):
-        w1_copy(j).start()
+    def w5_copy(m):
+        ref = wgrad.at[me.near_id()]
+        return remote(ref, ref, w5_send.at[m - 1], w5_recv.at[m - 1], me.near_peer(m))
+
+    for m in range(1, 8):
+        n1_copy(m).start()
+    n1[me.near_id()] = w0[me.near_id()]
+
+    def weight_over_a():
+        for m in range(1, 8):
+            n1_copy(m).wait()
+        total = n1[0]
+        for m in range(1, 8):
+            total = total + n1[m]
+        for a in range(4):
+            s1[a] = total[a * 8:(a + 1) * 8]
+        b1[...] = total[32:40]
+        for j in (1, 2, 3):
+            w2_copy(j).start()
+            x1_copy(j).start()
+        w2[me.a] = s1[me.a]
+        x1[me.x] = b1[...]
+
+    def weight_over_b():
+        for j in (1, 2, 3):
+            w2_copy(j).wait()
+            x1_copy(j).wait()
+        s2[...] = w2[0] + w2[1] + w2[2] + w2[3]
+        b2[...] = x1[0] + x1[1] + x1[2] + x1[3]
+        for j in (1, 2, 3):
+            w3_copy(j).start()
+            z1_copy(j).start()
+        w3[me.b] = s2[...]
+        z1[me.z] = b2[...]
+
+    def weight_back_a():
+        for j in (1, 2, 3):
+            w3_copy(j).wait()
+            z1_copy(j).wait()
+        s4[me.a] = w3[0] + w3[1] + w3[2] + w3[3]
+        bgrad[...] = (z1[0] + z1[1] + z1[2] + z1[3])[:1]
+        for j in (1, 2, 3):
+            w4_copy(j).start()
+
+    def weight_back_near():
+        for j in (1, 2, 3):
+            w4_copy(j).wait()
+        wgrad[me.near_id()] = s4[...].reshape(32, WIDTH)
+        for m in range(1, 8):
+            w5_copy(m).start()
 
     for t in range(4):
         share_near(t).wait_recv()
@@ -279,24 +350,16 @@
     def products(k, j):
         yh, a = place(k)
         section = me.section(yh, a, (me.b + j) % 4)
-        sources = jnp.concatenate([back[rows[section, t]] for t in range(SLOTS)], axis=0)
+        sources = jnp.concatenate([back[rows[t, section]] for t in range(SLOTS)], axis=0)
         terms[j, k] = lax.dot_general(
             masked(values, section, picks, counts), sources, (((0,), (0,)), ((), ())),
             preferred_element_type=F32,
         ).astype(BF)
 
-    def contribute(k, carry):
+    def contribute(k):
         for j in (1, 3, 2):
             products(k, j)
             send_b(k, j).start()
-        return carry
-
-    def keep(k, carry):
-        products(k, 0)
-        return carry
-
-    lax.fori_loop(0, 8, contribute, 0)
-    lax.fori_loop(0, 8, keep, 0)
 
     def send_y(k):
         return remote(to_y.at[k], from_y.at[k], y_send.at[k], y_recv.at[k], me.y_peer())
@@ -311,9 +374,9 @@
         for source in range(4):
             for p in range(2):
                 if source == 0:
-                    hit, tile = pulls[section, p] == q, terms[0, k, p * TILE:(p + 1) * TILE]
+                    hit, tile = pulls[p, section] == q, terms[0, k, p * TILE:(p + 1) * TILE]
                 else:
-                    hit = wants[source - 1, section, p] == q
+                    hit = wants[source - 1, p, section] == q
                     tile = from_b[source - 1, k, p * TILE:(p + 1) * TILE]
                 sums += tile.astype(F32) * jnp.where(hit, jnp.float32(1), jnp.float32(0))
         return sums
@@ -322,7 +385,12 @@
         for j in (1, 2, 3):
             send_b(k, j).wait_recv()
 
-    def other_half(k):
+    def start(k, carry):
+        contribute(k)
+        return carry
+
+    def other_half(k, carry):
+        products(k, 0)
         arrive_b(k)
 
         def column(q, inner):
@@ -331,65 +399,45 @@
 
         lax.fori_loop(0, 4, column, 0)
         send_y(k).start()
-
-    def this_half(k):
+        contribute(4 + k)
+        pl.when(k == 0)(weight_over_a)
+        pl.when(k == 2)(weight_over_b)
+        return carry
+
+    def this_half(k, carry):
+        products(4 + k, 0)
         arrive_b(4 + k)
         send_y(k).wait_recv()
 
         def column(q, inner):
             sums = gather_b(4 + k, q) + from_y[k, q].astype(F32)
-            if k < 3:
-                to_a[k, q] = sums.astype(BF)
-            else:
-                held[q] = sums
+            to_a[k, q] = sums.astype(BF)
+            held[q] = sums
             return inner
 
         lax.fori_loop(0, 4, column, 0)
-        if k < 3:
+
+        @pl.when(k < 3)
+        def _():
             send_a(k).start()
 
-    other_half(0)
-    for j in (1, 2, 3):
-        w1_copy(j).wait()
-    s1[...] = w0[me.b] + w1[0] + w1[1] + w1[2]
-    for j in (1, 2, 3):
-        w2_copy(j).start()
-    other_half(1)
-    other_half(2)
-    for j in (1, 2, 3):
-        w2_copy(j).wait()
-    s2[...] = s1[me.a] + w2[0] + w2[1] + w2[2]
+        pl.when(k == 0)(weight_back_a)
+        pl.when(k == 2)(weight_back_near)
+        return carry
+
+    lax.fori_loop(0, 4, start, 0)
+    lax.fori_loop(0, 4, other_half, 0)
+    lax.fori_loop(0, 4, this_half, 0)
     for m in range(1, 8):
-        w3_copy(m).start()
-    w3[me.near_id()] = s2[...]
-    other_half(3)
-    this_half(0)
-    for m in range(1, 8):
-        w3_copy(m).wait()
-    total = w3[0]
-    for m in range(1, 8):
-        total = total + w3[m]
-    s4[me.a] = total
-    for j in (1, 2, 3):
-        w4_copy(j).start()
-    this_half(1)
-    this_half(2)
-    for j in (1, 2, 3):
-        w4_copy(j).wait()
-    for j in (1, 2, 3):
-        w5_copy(j).start()
-    w5[me.b] = s4[...]
-    this_half(3)
-    for j in (1, 2, 3):
-        w5_copy(j).wait()
-    for b in range(4):
-        for a in range(4):
-            wgrad[me.chunk(b, a)] = w5[b, a, :16]
-    bgrad[...] = w5[0, 0, 16:17]
+        w5_copy(m).wait()
+    give_wgrad = pltpu.make_async_copy(wgrad, wgrad_out, wgrad_sem)
+    give_wgrad.start()
     for k in range(3):
         send_a(k).wait_recv()
     for q in range(4):
         fgrad[q] = held[q] + from_a[0, q].astype(F32) + from_a[1, q].astype(F32) + from_a[2, q].astype(F32)
+    give_fgrad = pltpu.make_async_copy(fgrad, fgrad_out, fgrad_sem)
+    give_fgrad.start()
 
     for j in (1, 2, 3):
         along(j).wait_send()
@@ -410,6 +458,9 @@
         return carry
 
     lax.fori_loop(0, 8, drain, 0)
+    give_act.wait()
+    give_wgrad.wait()
+    give_fgrad.wait()
 
 
 def layer(features, values, weight, bias, cotangent, rows, picks, counts, pulls):
@@ -422,16 +473,18 @@
         out_shape=(
             jax.ShapeDtypeStruct((4, TILE, WIDTH), BF),
             jax.ShapeDtypeStruct((4, TILE, WIDTH), F32),
-            jax.ShapeDtypeStruct((16, 16, WIDTH), F32),
+            jax.ShapeDtypeStruct((8, 32, WIDTH), F32),
             jax.ShapeDtypeStruct((1, WIDTH), F32),
         ),
-        in_specs=[hbm, hbm, vmem, vmem, vmem, vmem, smem, smem, smem, smem],
-        out_specs=(vmem,) * 4,
+        in_specs=[hbm, hbm, hbm, vmem, hbm, vmem, smem, smem, smem, smem],
+        out_specs=(hbm, hbm, hbm, vmem),
         scratch_shapes=[
             *[pltpu.VMEM((4, TILE, WIDTH), BF)] * 8,
             pltpu.VMEM((SECTIONS, SLOTS, TILE, TILE), BF),
-            pltpu.VMEM((3, SECTIONS, 2), jnp.int32),
-            pltpu.SMEM((3, SECTIONS, 2), jnp.int32),
+            pltpu.VMEM((WIDTH, WIDTH), BF),
+            pltpu.VMEM((4, TILE, WIDTH), BF),
+            pltpu.VMEM((3, 2, SECTIONS), jnp.int32),
+            pltpu.SMEM((3, 2, SECTIONS), jnp.int32),
             pltpu.VMEM((3, 8, 2, TILE, WIDTH), BF),
             pltpu.VMEM((4, 8, 2, TILE, WIDTH), BF),
             pltpu.VMEM((129, TILE, WIDTH), F32),
@@ -440,28 +493,37 @@
             pltpu.VMEM((2, 4, TILE, WIDTH), F32),
             pltpu.VMEM((4, TILE, WIDTH), BF),
             pltpu.VMEM((4, TILE, WIDTH), BF),
+            pltpu.VMEM((QUARTER, WIDTH), BF),
+            pltpu.VMEM((QUARTER, WIDTH), BF),
+            pltpu.VMEM((4, TILE, WIDTH), BF),
             pltpu.VMEM((16, TILE, WIDTH), BF),
             pltpu.VMEM((4, 8, 2 * TILE, WIDTH), BF),
             pltpu.VMEM((3, 8, 2 * TILE, WIDTH), BF),
             pltpu.VMEM((4, 4, TILE, WIDTH), BF),
             pltpu.VMEM((4, 4, TILE, WIDTH), BF),
-            pltpu.VMEM((3, 4, TILE, WIDTH), BF),
+            pltpu.VMEM((4, 4, TILE, WIDTH), BF),
             pltpu.VMEM((3, 4, TILE, WIDTH), BF),
             pltpu.VMEM((4, TILE, WIDTH), F32),
-            pltpu.VMEM((4, 4, 24, WIDTH), F32),
-            pltpu.VMEM((3, 4, 24, WIDTH), F32),
-            pltpu.VMEM((4, 24, WIDTH), F32),
-            pltpu.VMEM((3, 24, WIDTH), F32),
-            pltpu.VMEM((24, WIDTH), F32),
-            pltpu.VMEM((8, 24, WIDTH), F32),
-            pltpu.VMEM((4, 24, WIDTH), F32),
-            pltpu.VMEM((4, 4, 24, WIDTH), F32),
-            dma, dma, dma, dma((3,)), dma((3,)),
+            pltpu.VMEM((4, TILE, WIDTH), F32),
+            pltpu.VMEM((8, 40, WIDTH), F32),
+            pltpu.VMEM((8, 40, WIDTH), F32),
+            pltpu.VMEM((4, 8, WIDTH), F32),
+            pltpu.VMEM((4, 8, WIDTH), F32),
+            pltpu.VMEM((8, WIDTH), F32),
+            pltpu.VMEM((4, 8, WIDTH), F32),
+            pltpu.VMEM((4, 8, WIDTH), F32),
+            pltpu.VMEM((8, 32, WIDTH), F32),
+            pltpu.VMEM((8, WIDTH), F32),
+            pltpu.VMEM((4, 8, WIDTH), F32),
+            pltpu.VMEM((8, WIDTH), F32),
+            pltpu.VMEM((4, 8, WIDTH), F32),
+            *[dma] * 8, dma((3,)), dma((3,)),
             dma((3,)), dma((3,)), dma((4,)), dma((4,)), dma((3, 8)), dma((3, 8)),
             dma((2, 4)), dma((2, 4)), dma((4,)), dma((4,)),
             dma((4,)), dma((4,)), dma((4,)), dma((4,)), dma((4,)), dma((4,)),
             dma((3, 8)), dma((3, 8)), dma((4,)), dma((4,)), dma((3,)), dma((3,)),
-            dma((3,)), dma((3,)), dma((3,)), dma((3,)), dma((7,)), dma((7,)),
+            dma((7,)), dma((7,)), dma((3,)), dma((3,)), dma((3,)), dma((3,)),
+            dma((3,)), dma((3,)), dma((7,)), dma((7,)),
             dma((3,)), dma((3,)), dma((3,)), dma((3,)),
         ],
         compiler_params=pltpu.CompilerParams(
@@ -473,20 +535,47 @@
     )
 
 
+def hand_over_kernel(*refs):
+    into, out_of, sources, targets, held = refs[12], refs[13], refs[:4], refs[4:8], refs[8:12]
+    come = [pltpu.make_async_copy(sources[n], held[n], into.at[n]) for n in range(4)]
+    go = [pltpu.make_async_copy(held[n], targets[n], out_of.at[n]) for n in range(4)]
+    for copy in come:
+        copy.start()
+    for n in (0, 2, 3, 1):
+        come[n].wait()
+        go[n].start()
+    for copy in go:
+        copy.wait()
+
+
+def hand_over(*arrays):
+    hbm = pl.BlockSpec(memory_space=pl.ANY)
+    return pl.pallas_call(
+        hand_over_kernel,
+        name="hand_over",
+        out_shape=tuple(jax.ShapeDtypeStruct(array.shape, array.dtype) for array in arrays),
+        in_specs=[hbm] * 4,
+        out_specs=(hbm,) * 4,
+        scratch_shapes=[pltpu.VMEM(array.shape, array.dtype) for array in arrays]
+        + [pltpu.SemaphoreType.DMA((4,))] * 2,
+        compiler_params=pltpu.CompilerParams(vmem_limit_bytes=VMEM_LIMIT),
+    )(*arrays)
+
+
 def local(
     features, weight, bias, cotangent, tile_vals, tile_rows, tile_pick, tile_count, pull_cols
 ):
-    act, fgrad, wgrad, bgrad = layer(
+    act, fgrad, wgrad, bgrad = hand_over(*layer(
         features,
         tile_vals.reshape(SECTIONS, SLOTS, TILE, TILE),
         weight,
         bias,
         cotangent,
-        tile_rows.reshape(SECTIONS, SLOTS),
-        tile_pick.reshape(SECTIONS, SLOTS),
+        tile_rows.reshape(SECTIONS, SLOTS).T,
+        tile_pick.reshape(SECTIONS, SLOTS).T,
         tile_count.reshape(1, SECTIONS),
-        pull_cols.reshape(SECTIONS, 2),
-    )
+        pull_cols.reshape(SECTIONS, 2).T,
+    ))
     return (
         act.reshape(QUARTER, WIDTH),
         fgrad.reshape(QUARTER, WIDTH),

time: 114 us -> 98.1 us (0.86)
  local copies, waits for them, and re-layouts: 10.5 us -> 0 us
  Pallas kernels: 103 us -> 96.3 us
    pallas_call x1, Pallas kernels: 103 us -> 94.2 us  [layer(): pl.pallas_call(layer_kernel, name='layer', out_shape=(jax.ShapeDtypeStruc...]
    unnamed x4 -> x0, local copies, waits for them, and re-layouts: 6.45 us -> none
    reshape x3 -> x0, local copies, waits for them, and re-layouts: 4.1 us -> none  [the longest x1 1.37 us: local(): tile_rows.reshape(SECTIONS, SLOTS)]
    pallas_call x0 -> x1, Pallas kernels: none -> 2.14 us  [hand_over(): pl.pallas_call(hand_over_kernel, name='hand_over', out_shape=tuple((jax.S...]
where the time goes in v3:
time: 98.1 us; the launch traced here: 97 us
  Pallas kernels  96.3 us (98%)
    pallas_call x1, Pallas kernels, layer(): pl.pallas_call(layer_kernel, name='layer', out_shape=(jax.ShapeDtypeStruc...  94.2 us
    pallas_call x1, Pallas kernels, hand_over(): pl.pallas_call(hand_over_kernel, name='hand_over', out_shape=tuple((jax.S...  2.14 us

profile of v3, /device:TPU:0, one launch (start us, length us, event | category | flops | bytes accessed | tf_op | source)
XLA Modules:
  0.0 97.0 jit_solution(17659607723899339705)
XLA Ops:
  0.6 94.2 %layer.1 = (bf16[4,128,256]{2,1,0:T(8,128)(2,1)}, f32[4,128,256]{2,1,0:T(8,128)}, f32[8,32,256]{2,1,0:T(8,128)}, f32[1,256]{1,0:T(1,128)}) custom-call(bf16[16,128,256]{2,1,0:T(8,128)(2,1)} %bitcast.19, bf16[32,4,128,128]{3,2,1,0:T(8,128)(2,1)} %bitcast.18, bf16[256,256]{1,0:T(8,128)(2,1)} %weight_hbm.1, f32[1,256]{1,0:T(1,128)} %bitcast.25, ...), custom_call_target="tpu_custom_call" | custom-call | tf_op jit(solution)/shard_map/layer/pallas_call | solution.py:470
  94.8 2.1 %hand_over.1 = (bf16[4,128,256]{2,1,0:T(8,128)(2,1)}, f32[4,128,256]{2,1,0:T(8,128)}, f32[8,32,256]{2,1,0:T(8,128)}, f32[1,256]{1,0:T(1,128)}) custom-call(bf16[4,128,256]{2,1,0:T(8,128)(2,1)} %get-tuple-element.12.refs_0_, f32[4,128,256]{2,1,0:T(8,128)} %get-tuple-element.13.refs_1_, f32[8,32,256]{2,1,0:T(8,128)} %get-tuple-element.14.refs_2_, ...), custom_call_target="tpu_custom_call" | custom-call | tf_op jit(solution)/shard_map/hand_over/pallas_call | solution.py:553

commit v4 on v3

--- a/solution.py
+++ b/solution.py
@@ -87,16 +87,16 @@
 
 
 def layer_kernel(
-    features, values_hbm, weight_hbm, bias, cot_hbm, pull_vec, rows, picks, counts, pulls,
-    act_out, fgrad_out, wgrad_out, bgrad, *scratch,
+    features, values_hbm, weight_hbm, bias_hbm, cot_hbm, rows_hbm, picks_hbm, counts_hbm, pulls_hbm,
+    act_out, fgrad_out, wgrad_out, bgrad_out, *scratch,
 ):
     dense, scratch = scratch[:8], scratch[8:]
-    (values, weight, cotangent, asked, wants, packed, got, running, last,
+    (values, weight, bias, cotangent, rows, picks, counts, pulls, pull_vec, asked, wants, packed, got, running, last,
      swap_out, from_core, to_near, from_near, agg_all, slope_all, act, back,
      terms, from_b, to_y, from_y, to_a, from_a, held, fgrad,
-     w0, n1, s1, w2, s2, w3, s4, wgrad, b1, x1, b2, z1,
-     load_sem, weight_sem, cot_sem, own_sem, want_sem, act_sem, fgrad_sem, wgrad_sem, ask_send, ask_recv,
-     fa_send, fa_recv, fy_send, fy_recv, fb_send, fb_recv,
+     w0, n1, s1, w2, s2, w3, s4, wgrad, b1, x1, b2, z1, bgrad,
+     load_sem, own_sem, pull_sem, want_sem, act_sem, fgrad_sem, wgrad_sem, bgrad_sem, ask_send, ask_recv,
+     fa_send, fa_recv, fr_send, fr_recv, fy_send, fy_recv, fb_send, fb_recv,
      core_send, core_recv, near_send, near_recv,
      gc_send, gc_recv, gn_send, gn_recv, gf_send, gf_recv,
      b_send, b_recv, y_send, y_recv, a_send, a_recv,
@@ -107,10 +107,14 @@
         features.at[pl.ds((me.yl * 2 + me.core) * 4, 4)], dense[0], own_sem
     )
     fetch.start()
+    fetch_pull = pltpu.make_async_copy(pulls_hbm, pull_vec, pull_sem)
+    fetch_pull.start()
     loads = [
-        pltpu.make_async_copy(values_hbm, values, load_sem),
-        pltpu.make_async_copy(weight_hbm, weight, weight_sem),
-        pltpu.make_async_copy(cot_hbm, cotangent, cot_sem),
+        pltpu.make_async_copy(src, dst, load_sem.at[n])
+        for n, (src, dst) in enumerate([
+            (pulls_hbm, pulls), (rows_hbm, rows), (picks_hbm, picks), (counts_hbm, counts),
+            (values_hbm, values), (weight_hbm, weight), (bias_hbm, bias), (cot_hbm, cotangent),
+        ])
     ]
     for load in loads:
         load.start()
@@ -123,12 +127,19 @@
     def ask(j):
         return remote(pull_vec, asked.at[j - 1], ask_send.at[j - 1], ask_recv.at[j - 1], me.b_peer(j))
 
+    fetch_pull.wait()
     for j in (1, 2, 3):
         ask(j).start()
     fetch.wait()
 
     def along(j):
         return remote(dense[0], dense[j], fa_send.at[j - 1], fa_recv.at[j - 1], me.a_peer(j))
+
+    def relay(j):
+        half = pl.ds(j // 2 * 2, 2)
+        return remote(
+            dense[j].at[half], dense[2].at[half], fr_send.at[j // 2], fr_recv.at[j // 2], me.a_peer(j)
+        )
 
     def across(j):
         return remote(dense[j], dense[4 + j], fy_send.at[j], fy_recv.at[j], me.y_peer())
@@ -141,9 +152,10 @@
     def block_section(n, b):
         return me.section((me.yh + n // 4) % 2, (me.a + 4 - n % 4) % 4, b)
 
-    for j in (1, 3, 2):
+    for j in (1, 3):
         along(j).start()
     across(0).start()
+    loads[0].wait()
     for j in (1, 2, 3):
         ask(j).wait()
         table = pltpu.make_async_copy(asked.at[j - 1], wants.at[j - 1], want_sem)
@@ -161,15 +173,20 @@
             got[0, n, p] = dense[n][pulls[p, column]]
 
     serve(0)
-    for j in (1, 3, 2):
+    for j in (1, 3):
         along(j).wait_recv()
+        relay(j).start()
         across(j).start()
         serve(j)
+    for j in (1, 3):
+        relay(j).wait_recv()
+    across(2).start()
+    serve(2)
     for j in (0, 1, 3, 2):
         across(j).wait_recv()
         serve(4 + j)
 
-    for load in loads:
+    for load in loads[1:]:
         load.wait()
     running[128] = jnp.zeros((TILE, WIDTH), F32)
 
@@ -289,6 +306,8 @@
         n1_copy(m).start()
     n1[me.near_id()] = w0[me.near_id()]
 
+    give_bgrad = pltpu.make_async_copy(bgrad, bgrad_out, bgrad_sem)
+
     def weight_over_a():
         for m in range(1, 8):
             n1_copy(m).wait()
@@ -322,6 +341,7 @@
             z1_copy(j).wait()
         s4[me.a] = w3[0] + w3[1] + w3[2] + w3[3]
         bgrad[...] = (z1[0] + z1[1] + z1[2] + z1[3])[:1]
+        give_bgrad.start()
         for j in (1, 2, 3):
             w4_copy(j).start()
 
@@ -387,6 +407,7 @@
 
     def start(k, carry):
         contribute(k)
+        pl.when(k == 2)(weight_over_a)
         return carry
 
     def other_half(k, carry):
@@ -400,8 +421,8 @@
         lax.fori_loop(0, 4, column, 0)
         send_y(k).start()
         contribute(4 + k)
-        pl.when(k == 0)(weight_over_a)
-        pl.when(k == 2)(weight_over_b)
+        pl.when(k == 0)(weight_over_b)
+        pl.when(k == 2)(weight_back_a)
         return carry
 
     def this_half(k, carry):
@@ -421,8 +442,7 @@
         def _():
             send_a(k).start()
 
-        pl.when(k == 0)(weight_back_a)
-        pl.when(k == 2)(weight_back_near)
+        pl.when(k == 0)(weight_back_near)
         return carry
 
     lax.fori_loop(0, 4, start, 0)
@@ -439,8 +459,9 @@
     give_fgrad = pltpu.make_async_copy(fgrad, fgrad_out, fgrad_sem)
     give_fgrad.start()
 
-    for j in (1, 2, 3):
+    for j in (1, 3):
         along(j).wait_send()
+        relay(j).wait_send()
     for j in range(4):
         across(j).wait_send()
         over(j).wait_send()
@@ -459,13 +480,13 @@
 
     lax.fori_loop(0, 8, drain, 0)
     give_act.wait()
+    give_bgrad.wait()
     give_wgrad.wait()
     give_fgrad.wait()
 
 
 def layer(features, values, weight, bias, cotangent, rows, picks, counts, pulls):
     dma = pltpu.SemaphoreType.DMA
-    vmem, smem = pl.BlockSpec(memory_space=pltpu.VMEM), pl.BlockSpec(memory_space=pltpu.SMEM)
     hbm = pl.BlockSpec(memory_space=pl.ANY)
     return pl.pallas_call(
         layer_kernel,
@@ -476,13 +497,19 @@
             jax.ShapeDtypeStruct((8, 32, WIDTH), F32),
             jax.ShapeDtypeStruct((1, WIDTH), F32),
         ),
-        in_specs=[hbm, hbm, hbm, vmem, hbm, vmem, smem, smem, smem, smem],
-        out_specs=(hbm, hbm, hbm, vmem),
+        in_specs=[hbm] * 9,
+        out_specs=(hbm,) * 4,
         scratch_shapes=[
             *[pltpu.VMEM((4, TILE, WIDTH), BF)] * 8,
             pltpu.VMEM((SECTIONS, SLOTS, TILE, TILE), BF),
             pltpu.VMEM((WIDTH, WIDTH), BF),
+            pltpu.VMEM((1, WIDTH), F32),
             pltpu.VMEM((4, TILE, WIDTH), BF),
+            pltpu.SMEM((SLOTS, SECTIONS), jnp.int32),
+            pltpu.SMEM((SLOTS, SECTIONS), jnp.int32),
+            pltpu.SMEM((1, SECTIONS), jnp.int32),
+            pltpu.SMEM((2, SECTIONS), jnp.int32),
+            pltpu.VMEM((2, SECTIONS), jnp.int32),
             pltpu.VMEM((3, 2, SECTIONS), jnp.int32),
             pltpu.SMEM((3, 2, SECTIONS), jnp.int32),
             pltpu.VMEM((3, 8, 2, TILE, WIDTH), BF),
@@ -517,8 +544,9 @@
             pltpu.VMEM((4, 8, WIDTH), F32),
             pltpu.VMEM((8, WIDTH), F32),
             pltpu.VMEM((4, 8, WIDTH), F32),
-            *[dma] * 8, dma((3,)), dma((3,)),
-            dma((3,)), dma((3,)), dma((4,)), dma((4,)), dma((3, 8)), dma((3, 8)),
+            pltpu.VMEM((1, WIDTH), F32),
+            dma((8,)), *[dma] * 7, dma((3,)), dma((3,)),
+            dma((3,)), dma((3,)), dma((2,)), dma((2,)), dma((4,)), dma((4,)), dma((3, 8)), dma((3, 8)),
             dma((2, 4)), dma((2, 4)), dma((4,)), dma((4,)),
             dma((4,)), dma((4,)), dma((4,)), dma((4,)), dma((4,)), dma((4,)),
             dma((3, 8)), dma((3, 8)), dma((4,)), dma((4,)), dma((3,)), dma((3,)),
@@ -531,7 +559,7 @@
         ),
     )(
         features.reshape(16, TILE, WIDTH), values, weight, bias.reshape(1, WIDTH),
-        cotangent.reshape(4, TILE, WIDTH), pulls, rows, picks, counts, pulls,
+        cotangent.reshape(4, TILE, WIDTH), rows, picks, counts, pulls,
     )
 
 

time: 98.1 us -> 95.4 us (0.972)
  Pallas kernels: 96.3 us -> 94.3 us
    pallas_call x1, Pallas kernels: 94.2 us -> 92.1 us  [layer(): pl.pallas_call(layer_kernel, name='layer', out_shape=(jax.ShapeDtypeStruc...]
where the time goes in v4:
time: 95.4 us; the launch traced here: 94.9 us
  Pallas kernels  94.3 us (99%)
    pallas_call x1, Pallas kernels, layer(): pl.pallas_call(layer_kernel, name='layer', out_shape=(jax.ShapeDtypeStruc...  92.1 us
    pallas_call x1, Pallas kernels, hand_over(): pl.pallas_call(hand_over_kernel, name='hand_over', out_shape=tuple((jax.S...  2.14 us

profile of v4, /device:TPU:0, one launch (start us, length us, event | category | flops | bytes accessed | tf_op | source)
XLA Modules:
  0.0 94.9 jit_solution(15278378753696494771)
XLA Ops:
  0.6 92.1 %layer.1 = (bf16[4,128,256]{2,1,0:T(8,128)(2,1)}, f32[4,128,256]{2,1,0:T(8,128)}, f32[8,32,256]{2,1,0:T(8,128)}, f32[1,256]{1,0:T(1,128)}) custom-call(bf16[16,128,256]{2,1,0:T(8,128)(2,1)} %bitcast.19, bf16[32,4,128,128]{3,2,1,0:T(8,128)(2,1)} %bitcast.18, bf16[256,256]{1,0:T(8,128)(2,1)} %weight_hbm.1, f32[1,256]{1,0:T(1,128)} %bitcast.23, ...), custom_call_target="tpu_custom_call" | custom-call | tf_op jit(solution)/shard_map/layer/pallas_call | solution.py:491
  92.8 2.1 %hand_over.1 = (bf16[4,128,256]{2,1,0:T(8,128)(2,1)}, f32[4,128,256]{2,1,0:T(8,128)}, f32[8,32,256]{2,1,0:T(8,128)}, f32[1,256]{1,0:T(1,128)}) custom-call(bf16[4,128,256]{2,1,0:T(8,128)(2,1)} %get-tuple-element.12.refs_0_, f32[4,128,256]{2,1,0:T(8,128)} %get-tuple-element.13.refs_1_, f32[8,32,256]{2,1,0:T(8,128)} %get-tuple-element.14.refs_2_, ...), custom_call_target="tpu_custom_call" | custom-call | tf_op jit(solution)/shard_map/hand_over/pallas_call | solution.py:581

commit v5 on v4

--- a/solution.py
+++ b/solution.py
@@ -88,14 +88,14 @@
 
 def layer_kernel(
     features, values_hbm, weight_hbm, bias_hbm, cot_hbm, rows_hbm, picks_hbm, counts_hbm, pulls_hbm,
-    act_out, fgrad_out, wgrad_out, bgrad_out, *scratch,
+    act, fgrad, wgrad, bgrad, *scratch,
 ):
     dense, scratch = scratch[:8], scratch[8:]
     (values, weight, bias, cotangent, rows, picks, counts, pulls, pull_vec, asked, wants, packed, got, running, last,
-     swap_out, from_core, to_near, from_near, agg_all, slope_all, act, back,
-     terms, from_b, to_y, from_y, to_a, from_a, held, fgrad,
-     w0, n1, s1, w2, s2, w3, s4, wgrad, b1, x1, b2, z1, bgrad,
-     load_sem, own_sem, pull_sem, want_sem, act_sem, fgrad_sem, wgrad_sem, bgrad_sem, ask_send, ask_recv,
+     swap_out, from_core, to_near, from_near, agg_all, slope_all, back,
+     terms, from_b, to_y, from_y, to_a, from_a,
+     w0, n1, s1, w2, s2, w3, s4, b1, x1, b2, z1,
+     load_sem, own_sem, pull_sem, want_sem, ask_send, ask_recv,
      fa_send, fa_recv, fr_send, fr_recv, fy_send, fy_recv, fb_send, fb_recv,
      core_send, core_recv, near_send, near_recv,
      gc_send, gc_recv, gn_send, gn_recv, gf_send, gf_recv,
@@ -264,8 +264,6 @@
         ).astype(BF)
         share_near(t).start()
         share_core(t).start()
-    give_act = pltpu.make_async_copy(act, act_out, act_sem)
-    give_act.start()
 
     grad = lax.dot_general(
         agg_all[...], slope_all[...], (((0,), (0,)), ((), ())), preferred_element_type=F32
@@ -305,8 +303,6 @@
     for m in range(1, 8):
         n1_copy(m).start()
     n1[me.near_id()] = w0[me.near_id()]
-
-    give_bgrad = pltpu.make_async_copy(bgrad, bgrad_out, bgrad_sem)
 
     def weight_over_a():
         for m in range(1, 8):
@@ -341,7 +337,6 @@
             z1_copy(j).wait()
         s4[me.a] = w3[0] + w3[1] + w3[2] + w3[3]
         bgrad[...] = (z1[0] + z1[1] + z1[2] + z1[3])[:1]
-        give_bgrad.start()
         for j in (1, 2, 3):
             w4_copy(j).start()
 
@@ -359,8 +354,11 @@
         share_core(t).wait()
         forward_on(t).wait()
 
+    def step_a(k):
+        return 2 - k + k // 2 * 3 - k // 3 * 2
+
     def place(k):
-        return (me.yh + 1 + k // 4) % 2, (me.a + 1 + k % 4) % 4
+        return (me.yh + 1 + k // 4) % 2, (me.a + step_a(k % 4)) % 4
 
     def send_b(k, j):
         return remote(
@@ -385,7 +383,7 @@
         return remote(to_y.at[k], from_y.at[k], y_send.at[k], y_recv.at[k], me.y_peer())
 
     def send_a(k):
-        return remote(to_a.at[k], from_a.at[k], a_send.at[k], a_recv.at[k], me.a_peer(1 + k))
+        return remote(to_a.at[k], from_a.at[k], a_send.at[k], a_recv.at[k], me.a_peer(step_a(k)))
 
     def gather_b(k, q):
         yh, a = place(k)
@@ -411,6 +409,7 @@
         return carry
 
     def other_half(k, carry):
+        contribute(4 + k)
         products(k, 0)
         arrive_b(k)
 
@@ -420,7 +419,6 @@
 
         lax.fori_loop(0, 4, column, 0)
         send_y(k).start()
-        contribute(4 + k)
         pl.when(k == 0)(weight_over_b)
         pl.when(k == 2)(weight_back_a)
         return carry
@@ -431,33 +429,33 @@
         send_y(k).wait_recv()
 
         def column(q, inner):
-            sums = gather_b(4 + k, q) + from_y[k, q].astype(F32)
-            to_a[k, q] = sums.astype(BF)
-            held[q] = sums
+            to_a[k, q] = (gather_b(4 + k, q) + from_y[k, q].astype(F32)).astype(BF)
             return inner
 
         lax.fori_loop(0, 4, column, 0)
-
-        @pl.when(k < 3)
-        def _():
-            send_a(k).start()
-
+        send_a(k).start()
         pl.when(k == 0)(weight_back_near)
         return carry
 
     lax.fori_loop(0, 4, start, 0)
     lax.fori_loop(0, 4, other_half, 0)
-    lax.fori_loop(0, 4, this_half, 0)
+    lax.fori_loop(0, 3, this_half, 0)
+    products(7, 0)
+    arrive_b(7)
+    send_y(3).wait_recv()
+    for k in range(3):
+        send_a(k).wait_recv()
+
+    def own(q, carry):
+        fgrad[q] = gather_b(7, q) + sum(
+            (ref[n, q].astype(F32) for ref, n in ((from_y, 3), (from_a, 0), (from_a, 1), (from_a, 2))),
+            jnp.zeros((TILE, WIDTH), F32),
+        )
+        return carry
+
+    lax.fori_loop(0, 4, own, 0)
     for m in range(1, 8):
         w5_copy(m).wait()
-    give_wgrad = pltpu.make_async_copy(wgrad, wgrad_out, wgrad_sem)
-    give_wgrad.start()
-    for k in range(3):
-        send_a(k).wait_recv()
-    for q in range(4):
-        fgrad[q] = held[q] + from_a[0, q].astype(F32) + from_a[1, q].astype(F32) + from_a[2, q].astype(F32)
-    give_fgrad = pltpu.make_async_copy(fgrad, fgrad_out, fgrad_sem)
-    give_fgrad.start()
 
     for j in (1, 3):
         along(j).wait_send()
@@ -479,10 +477,6 @@
         return carry
 
     lax.fori_loop(0, 8, drain, 0)
-    give_act.wait()
-    give_bgrad.wait()
-    give_wgrad.wait()
-    give_fgrad.wait()
 
 
 def layer(features, values, weight, bias, cotangent, rows, picks, counts, pulls):
@@ -492,13 +486,13 @@
         layer_kernel,
         name="layer",
         out_shape=(
-            jax.ShapeDtypeStruct((4, TILE, WIDTH), BF),
-            jax.ShapeDtypeStruct((4, TILE, WIDTH), F32),
-            jax.ShapeDtypeStruct((8, 32, WIDTH), F32),
-            jax.ShapeDtypeStruct((1, WIDTH), F32),
+            pltpu.VMEM((4, TILE, WIDTH), BF),
+            pltpu.VMEM((4, TILE, WIDTH), F32),
+            pltpu.VMEM((8, 32, WIDTH), F32),
+            pltpu.VMEM((1, WIDTH), F32),
         ),
         in_specs=[hbm] * 9,
-        out_specs=(hbm,) * 4,
+        out_specs=(pl.BlockSpec(memory_space=pltpu.VMEM),) * 4,
         scratch_shapes=[
             *[pltpu.VMEM((4, TILE, WIDTH), BF)] * 8,
             pltpu.VMEM((SECTIONS, SLOTS, TILE, TILE), BF),
@@ -522,7 +516,6 @@
             pltpu.VMEM((4, TILE, WIDTH), BF),
             pltpu.VMEM((QUARTER, WIDTH), BF),
             pltpu.VMEM((QUARTER, WIDTH), BF),
-            pltpu.VMEM((4, TILE, WIDTH), BF),
             pltpu.VMEM((16, TILE, WIDTH), BF),
             pltpu.VMEM((4, 8, 2 * TILE, WIDTH), BF),
             pltpu.VMEM((3, 8, 2 * TILE, WIDTH), BF),
@@ -530,8 +523,6 @@
             pltpu.VMEM((4, 4, TILE, WIDTH), BF),
             pltpu.VMEM((4, 4, TILE, WIDTH), BF),
             pltpu.VMEM((3, 4, TILE, WIDTH), BF),
-            pltpu.VMEM((4, TILE, WIDTH), F32),
-            pltpu.VMEM((4, TILE, WIDTH), F32),
             pltpu.VMEM((8, 40, WIDTH), F32),
             pltpu.VMEM((8, 40, WIDTH), F32),
             pltpu.VMEM((4, 8, WIDTH), F32),
@@ -539,13 +530,11 @@
             pltpu.VMEM((8, WIDTH), F32),
             pltpu.VMEM((4, 8, WIDTH), F32),
             pltpu.VMEM((4, 8, WIDTH), F32),
-            pltpu.VMEM((8, 32, WIDTH), F32),
             pltpu.VMEM((8, WIDTH), F32),
             pltpu.VMEM((4, 8, WIDTH), F32),
             pltpu.VMEM((8, WIDTH), F32),
             pltpu.VMEM((4, 8, WIDTH), F32),
-            pltpu.VMEM((1, WIDTH), F32),
-            dma((8,)), *[dma] * 7, dma((3,)), dma((3,)),
+            dma((8,)), *[dma] * 3, dma((3,)), dma((3,)),
             dma((3,)), dma((3,)), dma((2,)), dma((2,)), dma((4,)), dma((4,)), dma((3, 8)), dma((3, 8)),
             dma((2, 4)), dma((2, 4)), dma((4,)), dma((4,)),
             dma((4,)), dma((4,)), dma((4,)), dma((4,)), dma((4,)), dma((4,)),
@@ -564,29 +553,24 @@
 
 
 def hand_over_kernel(*refs):
-    into, out_of, sources, targets, held = refs[12], refs[13], refs[:4], refs[4:8], refs[8:12]
-    come = [pltpu.make_async_copy(sources[n], held[n], into.at[n]) for n in range(4)]
-    go = [pltpu.make_async_copy(held[n], targets[n], out_of.at[n]) for n in range(4)]
-    for copy in come:
+    sems = refs[8]
+    copies = [pltpu.make_async_copy(refs[n], refs[4 + n], sems.at[n]) for n in range(4)]
+    for copy in copies:
         copy.start()
-    for n in (0, 2, 3, 1):
-        come[n].wait()
-        go[n].start()
-    for copy in go:
+    for copy in copies:
         copy.wait()
 
 
 def hand_over(*arrays):
-    hbm = pl.BlockSpec(memory_space=pl.ANY)
+    hbm, vmem = pl.BlockSpec(memory_space=pl.ANY), pl.BlockSpec(memory_space=pltpu.VMEM)
     return pl.pallas_call(
         hand_over_kernel,
         name="hand_over",
         out_shape=tuple(jax.ShapeDtypeStruct(array.shape, array.dtype) for array in arrays),
-        in_specs=[hbm] * 4,
+        in_specs=[vmem] * 4,
         out_specs=(hbm,) * 4,
-        scratch_shapes=[pltpu.VMEM(array.shape, array.dtype) for array in arrays]
-        + [pltpu.SemaphoreType.DMA((4,))] * 2,
-        compiler_params=pltpu.CompilerParams(vmem_limit_bytes=VMEM_LIMIT),
+        scratch_shapes=[pltpu.SemaphoreType.DMA((4,))],
+        compiler_params=pltpu.CompilerParams(vmem_limit_bytes=4 << 20),
     )(*arrays)
 
 

time: 95.4 us -> 93.5 us (0.980)
  Pallas kernels: 94.3 us -> 92.3 us
    pallas_call x1, Pallas kernels: 2.14 us -> 1 us  [hand_over(): pl.pallas_call(hand_over_kernel, name='hand_over', out_shape=tuple((jax.S...]
where the time goes in v5:
time: 93.5 us; the launch traced here: 93 us
  Pallas kernels  92.3 us (99%)
    pallas_call x1, Pallas kernels, layer(): pl.pallas_call(layer_kernel, name='layer', out_shape=(pltpu.VMEM((4, TILE...  91.3 us

profile of v5, /device:TPU:0, one launch (start us, length us, event | category | flops | bytes accessed | tf_op | source)
XLA Modules:
  0.0 93.0 jit_solution(251645883297358603)
XLA Ops:
  0.6 91.3 %layer.1 = (bf16[4,128,256]{2,1,0:T(8,128)(2,1)S(1)}, f32[4,128,256]{2,1,0:T(8,128)S(1)}, f32[8,32,256]{2,1,0:T(8,128)S(1)}, f32[1,256]{1,0:T(1,128)S(1)}) custom-call(bf16[16,128,256]{2,1,0:T(8,128)(2,1)} %bitcast.19, bf16[32,4,128,128]{3,2,1,0:T(8,128)(2,1)} %bitcast.18, bf16[256,256]{1,0:T(8,128)(2,1)} %weight_hbm.1, f32[1,256]{1,0:T(1,128)} %bitcast.23, ...), custom_call_target="tpu_custom_call" | custom-call | tf_op jit(solution)/shard_map/layer/pallas_call | solution.py:485
  92.0 1.0 %hand_over.1 = (bf16[4,128,256]{2,1,0:T(8,128)(2,1)}, f32[4,128,256]{2,1,0:T(8,128)}, f32[8,32,256]{2,1,0:T(8,128)}, f32[1,256]{1,0:T(1,128)}) custom-call(bf16[4,128,256]{2,1,0:T(8,128)(2,1)S(1)} %get-tuple-element.12.refs_0_, f32[4,128,256]{2,1,0:T(8,128)S(1)} %get-tuple-element.13.refs_1_, f32[8,32,256]{2,1,0:T(8,128)S(1)} %get-tuple-element.14.refs_2_, ...), custom_call_target="tpu_custom_call" | custom-call | tf_op jit(solution)/shard_map/hand_over/pallas_call | solution.py:566

commit v6 on v5

--- a/solution.py
+++ b/solution.py
@@ -177,6 +177,7 @@
         along(j).wait_recv()
         relay(j).start()
         across(j).start()
+    for j in (1, 3):
         serve(j)
     for j in (1, 3):
         relay(j).wait_recv()
@@ -225,14 +226,18 @@
     def over(t):
         return remote(to_near.at[t], from_near.at[t], near_send.at[t], near_recv.at[t], near_peer)
 
-    for n in range(2):
-        for t in range(4):
-            swap_out[n, t] = part((quarters[n] + 1 - me.core) * 4 + t)
-            swap(n, t).start()
+    def swap_start(n, t):
+        swap_out[n, t] = part((quarters[n] + 1 - me.core) * 4 + t)
+        swap(n, t).start()
+
+    for t in range(4):
+        swap_start(0, t)
     for t in range(4):
         swap(0, t).wait_recv()
         to_near[t] = (part((quarters[0] + me.core) * 4 + t) + from_core[0, t]).astype(BF)
         over(t).start()
+    for t in range(4):
+        swap_start(1, t)
 
     mine = me.yl * 2 + me.core
     yours = (1 - me.yl) * 2 + me.core

time: 93.5 us -> 93.3 us (level)
  no operation moved by 1% of the time
where the time goes in v6:
time: 93.3 us; the launch traced here: 92.9 us
  Pallas kernels  92.2 us (99%)
    pallas_call x1, Pallas kernels, layer(): pl.pallas_call(layer_kernel, name='layer', out_shape=(pltpu.VMEM((4, TILE...  91.2 us

profile of v6, /device:TPU:0, one launch (start us, length us, event | category | flops | bytes accessed | tf_op | source)
XLA Modules:
  0.0 92.9 jit_solution(10729665523334623708)
XLA Ops:
  0.6 91.2 %layer.1 = (bf16[4,128,256]{2,1,0:T(8,128)(2,1)S(1)}, f32[4,128,256]{2,1,0:T(8,128)S(1)}, f32[8,32,256]{2,1,0:T(8,128)S(1)}, f32[1,256]{1,0:T(1,128)S(1)}) custom-call(bf16[16,128,256]{2,1,0:T(8,128)(2,1)} %bitcast.19, bf16[32,4,128,128]{3,2,1,0:T(8,128)(2,1)} %bitcast.18, bf16[256,256]{1,0:T(8,128)(2,1)} %weight_hbm.1, f32[1,256]{1,0:T(1,128)} %bitcast.23, ...), custom_call_target="tpu_custom_call" | custom-call | tf_op jit(solution)/shard_map/layer/pallas_call | solution.py:490
  91.9 1.0 %hand_over.1 = (bf16[4,128,256]{2,1,0:T(8,128)(2,1)}, f32[4,128,256]{2,1,0:T(8,128)}, f32[8,32,256]{2,1,0:T(8,128)}, f32[1,256]{1,0:T(1,128)}) custom-call(bf16[4,128,256]{2,1,0:T(8,128)(2,1)S(1)} %get-tuple-element.12.refs_0_, f32[4,128,256]{2,1,0:T(8,128)S(1)} %get-tuple-element.13.refs_1_, f32[8,32,256]{2,1,0:T(8,128)S(1)} %get-tuple-element.14.refs_2_, ...), custom_call_target="tpu_custom_call" | custom-call | tf_op jit(solution)/shard_map/hand_over/pallas_call | solution.py:571

commit v7 on v5

--- a/solution.py
+++ b/solution.py
@@ -409,7 +409,10 @@
         return carry
 
     def other_half(k, carry):
-        contribute(4 + k)
+        @pl.when(k + 3 < 8)
+        def _():
+            contribute(3 + k)
+
         products(k, 0)
         arrive_b(k)
 
@@ -424,6 +427,10 @@
         return carry
 
     def this_half(k, carry):
+        @pl.when(k + 4 + 3 < 8)
+        def _():
+            contribute(4 + 3 + k)
+
         products(4 + k, 0)
         arrive_b(4 + k)
         send_y(k).wait_recv()
@@ -437,7 +444,7 @@
         pl.when(k == 0)(weight_back_near)
         return carry
 
-    lax.fori_loop(0, 4, start, 0)
+    lax.fori_loop(0, 3, start, 0)
     lax.fori_loop(0, 4, other_half, 0)
     lax.fori_loop(0, 3, this_half, 0)
     products(7, 0)

time: 93.5 us -> 93.5 us (level)
  no operation moved by 1% of the time
where the time goes in v7:
time: 93.5 us; the launch traced here: 93 us
  Pallas kernels  92.3 us (99%)
    pallas_call x1, Pallas kernels, layer(): pl.pallas_call(layer_kernel, name='layer', out_shape=(pltpu.VMEM((4, TILE...  91.3 us

profile of v7, /device:TPU:0, one launch (start us, length us, event | category | flops | bytes accessed | tf_op | source)
XLA Modules:
  0.0 93.0 jit_solution(3849943227447676008)
XLA Ops:
  0.6 91.3 %layer.1 = (bf16[4,128,256]{2,1,0:T(8,128)(2,1)S(1)}, f32[4,128,256]{2,1,0:T(8,128)S(1)}, f32[8,32,256]{2,1,0:T(8,128)S(1)}, f32[1,256]{1,0:T(1,128)S(1)}) custom-call(bf16[16,128,256]{2,1,0:T(8,128)(2,1)} %bitcast.19, bf16[32,4,128,128]{3,2,1,0:T(8,128)(2,1)} %bitcast.18, bf16[256,256]{1,0:T(8,128)(2,1)} %weight_hbm.1, f32[1,256]{1,0:T(1,128)} %bitcast.23, ...), custom_call_target="tpu_custom_call" | custom-call | tf_op jit(solution)/shard_map/layer/pallas_call | solution.py:492
  92.0 1.0 %hand_over.1 = (bf16[4,128,256]{2,1,0:T(8,128)(2,1)}, f32[4,128,256]{2,1,0:T(8,128)}, f32[8,32,256]{2,1,0:T(8,128)}, f32[1,256]{1,0:T(1,128)}) custom-call(bf16[4,128,256]{2,1,0:T(8,128)(2,1)S(1)} %get-tuple-element.12.refs_0_, f32[4,128,256]{2,1,0:T(8,128)S(1)} %get-tuple-element.13.refs_1_, f32[8,32,256]{2,1,0:T(8,128)S(1)} %get-tuple-element.14.refs_2_, ...), custom_call_target="tpu_custom_call" | custom-call | tf_op jit(solution)/shard_map/hand_over/pallas_call | solution.py:573
